TPU v7x, 32 devices: a whole 2x2x4 slice. The times are simulated.
32 devices in a mesh: dp: 16 (over z, x, core), tensor: 2 (over y).
Axes of the slice: x: 2, y: 2, z: 4, core: 2. Of those that a mesh axis runs over, the one named last changes fastest.
Arguments:
- tokens: bfloat16 [64, 502, 768], P('dp', 'tensor'), may hold values from -6 to 6
- slot_position: int32 [64], P('dp'), may hold values from -1 to 3, as said below
- cotangent: bfloat16 [64, 502, 768], P('dp', 'tensor'), may hold values from -6 to 6
- attention: float32 [4, 768, 768], P(None, 'dp', 'tensor'), may hold values from -4 to 4, as said below
- feedforward: float32 [2, 768, 3072], P(None, None, ('dp', 'tensor')), may hold values from -0.21875 to 0.21875
- vectors: float32 [16896], P(('dp', 'tensor')), may hold values from -6 to 6, as said below
- attn_momentum: float32 [4, 768, 768], P(None, 'dp', 'tensor'), may hold values from -2 to 2, as said below
- ffn_momentum: float32 [2, 768, 3072], P(None, None, ('dp', 'tensor')), may hold values from -3 to 3
- vec_momentum: float32 [16896], P(('dp', 'tensor')), may hold values from -3 to 3
- attn_average: float32 [4, 768, 768], P(None, 'dp', 'tensor'), may hold values from -4 to 4, as said below
- ffn_average: float32 [2, 768, 3072], P(None, None, ('dp', 'tensor')), may hold values from -0.21875 to 0.21875
- vec_average: float32 [16896], P(('dp', 'tensor')), may hold values from -6 to 6, as said below
Outputs:
- activations: bfloat16 [64, 502, 768], P('dp', 'tensor')
- token_grad: bfloat16 [64, 502, 768], P('dp', 'tensor')
- momentum_attn: float32 [4, 768, 768], P(None, 'dp', 'tensor')
- momentum_ffn: float32 [2, 768, 3072], P(None, None, ('dp', 'tensor'))
- momentum_vec: float32 [16896], P(('dp', 'tensor'))
- updated_attn: float32 [4, 768, 768], P(None, 'dp', 'tensor')
- updated_ffn: float32 [2, 768, 3072], P(None, None, ('dp', 'tensor'))
- updated_vec: float32 [16896], P(('dp', 'tensor'))
- averaged_attn: float32 [4, 768, 768], P(None, 'dp', 'tensor')
- averaged_ffn: float32 [2, 768, 3072], P(None, None, ('dp', 'tensor'))
- averaged_vec: float32 [16896], P(('dp', 'tensor'))
Inputs may be any that keep to these rules, and one draw needn't show every extreme that they name: `slot_position`: each bucket of 4 slots holds whole sequences one after another from its first slot: a slot holds its segment's place in its sequence, a sequence has 2 to 4 segments in consecutive slots starting at place 0, and the slots after a bucket's last sequence hold -1. Some bucket begins with a sequence of 4 segments. `attention`: entries of mean 0; the output projection's entries are larger than the others. `attn_momentum`: no entry is 0. `vectors`: gains near 1, biases of mean 0, initial memory of order one. `attn_average`: drawn by the same law as the attention weights. `vec_average`: drawn by the same law as vectors.
All inputs are finite; a program needn't handle non-finite values.
Results may differ from a plain program's by a relative error of at most 0.023.
Values may be sent and summed in bfloat16 or wider, within the bound.
A program may use at most 256 MiB of HBM per device.

v0:
```python
import functools
import math

import jax
import jax.numpy as jnp
from jax import lax
from jax.experimental import pallas as pl
from jax.experimental.pallas import tpu as pltpu
from jax.sharding import PartitionSpec as P

D = 768
HEADS = 12
DH = 64
FF = 3072
MEM = 10
SLOTS = 4
ROWS = 522
NVEC = 22

HALF = D // 2
SEG = ROWS - MEM
THIN = 16
LOCAL = 2
TILE = 256

EPSILON = 1e-05
MOMENTUM = 0.9
AVERAGE_DECAY = 0.75
ATTENTION_RATE = 0.06
FEEDFORWARD_RATE = 0.02
VECTOR_RATE = 0.1
MASK_VALUE = -1e30
SCALE = 1.0 / math.sqrt(DH)

F32 = jnp.float32
BF16 = jnp.bfloat16
MIB = 1 << 20

QUERY_BIAS, VALUE_BIAS, OUT_BIAS, GAIN1, SHIFT1, DOWN_BIAS, GAIN2, SHIFT2, UP_BIAS = range(9)
FIRST_MEMORY = UP_BIAS + FF // D


def nn(a, b):
    return lax.dot_general(a, b, (((1,), (0,)), ((), ())), preferred_element_type=F32)


def nt(a, b):
    return lax.dot_general(a, b, (((1,), (1,)), ((), ())), preferred_element_type=F32)


def tn(a, b):
    return lax.dot_general(a, b, (((0,), (0,)), ((), ())), preferred_element_type=F32)


def normalized(rows):
    center = rows - jnp.mean(rows, axis=-1, keepdims=True)
    spread = jnp.mean(center * center, axis=-1, keepdims=True)
    inverse = lax.rsqrt(spread + EPSILON)
    return center * inverse, inverse


def normalized_back(grad, unit, inverse):
    mean_grad = jnp.mean(grad, axis=-1, keepdims=True)
    mean_along = jnp.mean(grad * unit, axis=-1, keepdims=True)
    return inverse * (grad - mean_grad - unit * mean_along)


def gelu_parts(u):
    size = jnp.abs(u)
    t = 1.0 / (1.0 + (0.3275911 / math.sqrt(2.0)) * size)
    bell = jnp.exp(-0.5 * u * u)
    poly = t * (
        0.5 * 0.254829592
        + t
        * (
            0.5 * -0.284496736
            + t * (0.5 * 1.421413741 + t * (0.5 * -1.453152027 + t * (0.5 * 1.061405429)))
        )
    )
    tail = poly * bell
    cdf = jnp.where(u < 0, tail, 1.0 - tail)
    return u * cdf, cdf + (u * (1.0 / math.sqrt(2.0 * math.pi))) * bell


def row_sum(block):
    return jnp.sum(block, axis=0, keepdims=True)


def params(limit=60, **more):
    return pltpu.CompilerParams(vmem_limit_bytes=limit * MIB, **more)


def once(shape, index):
    return pl.BlockSpec(shape, lambda *_: index, pipeline_mode=pl.Buffered(1))


ANY = pl.BlockSpec(memory_space=pltpu.HBM)
SMEM = pl.BlockSpec(memory_space=pltpu.SMEM)
VMEM = pl.BlockSpec(memory_space=pltpu.VMEM)


def sds(shape, dtype):
    return jax.ShapeDtypeStruct(shape, dtype)


def my_place():
    dp = lax.axis_index("dp")
    return dp // 4, (dp // 2) % 2, dp % 2, lax.axis_index("tensor")


def device(z, x, c, y):
    return {"dp": (z * 2 + x) * 2 + c, "tensor": y}


def entry_barrier(nz):
    z, x, c, y = my_place()
    barrier = pltpu.get_barrier_semaphore()
    signal = lambda d: pl.semaphore_signal(
        barrier, inc=1, device_id=d, device_id_type=pl.DeviceIdType.MESH
    )
    signal(device(z, 1 - x, c, y))
    signal(device(z, x, 1 - c, y))
    signal(device(z, x, c, 1 - y))

    @pl.when(z > 0)
    def _():
        signal(device(z - 1, x, c, y))

    @pl.when(z < nz - 1)
    def _():
        signal(device(z + 1, x, c, y))

    up = lax.convert_element_type(z < nz - 1, jnp.int32)
    down = lax.convert_element_type(z > 0, jnp.int32)
    pl.semaphore_wait(barrier, 3 + up + down)


def attn_view(ref, z, x, c, y):
    return ref.at[:, z, x, c, :, pl.ds(pl.multiple_of(y * HALF, HALF), HALF)]


def ffn_view(ref, z, x, c, y):
    return ref.at[:, z, x, c, y]


def vec_view(ref, z, x, c, y):
    return ref.at[z, x, c, y]


def hidden_view(ref, z, x, c, y):
    return ref.at[z, x, c, y]


def partners(place, lead):
    _, x, _, y = place
    first = (x + (1 - lead) * (1 - 2 * x), y + lead * (1 - 2 * y))
    second = (x + lead * (1 - 2 * x), y + (1 - lead) * (1 - 2 * y))
    return first, second, (1 - x, 1 - y)


COLUMN, FIRST, SECOND, BOTH, CORE = 0, 1, 2, 3, 4
UP, DOWN, UP_FIRST, DOWN_FIRST = 0, 8, 9, 10


def remote(src, dst, send_sem, recv_sem, target):
    return pltpu.make_async_remote_copy(
        src_ref=src,
        dst_ref=dst,
        send_sem=send_sem,
        recv_sem=recv_sem,
        device_id=target,
        device_id_type=pl.DeviceIdType.MESH,
    )


def gather_steps(nz, place, lead, z_second, pieces, send_sem, recv_sem):
    z, x, c, y = place
    first, second, both = partners(place, lead)
    to_first = device(z, first[0], c, first[1])
    to_second = device(z, second[0], c, second[1])
    to_core = device(z, x, 1 - c, y)

    def copies(send, recv, shard, target):
        return [
            remote(
                view(out, *shard),
                view(out, *shard),
                send_sem.at[send, shard[0], i],
                recv_sem.at[recv, shard[0], i],
                target,
            )
            for i, out, view in pieces
        ]

    def start(*args):
        for copy in copies(*args):
            copy.start()

    def arrived(*args):
        for copy in copies(*args):
            copy.wait_recv()

    def sent(*args):
        for copy in copies(*args):
            copy.wait_send()

    def column(zz):
        return (zz, x, c, y)

    def of_first(zz):
        return (zz, first[0], c, first[1])

    def of_second(zz):
        return (zz, second[0], c, second[1])

    def of_both(zz):
        return (zz, both[0], c, both[1])

    core_first, core_second = CORE + 2 - lead, CORE + 1 + lead

    def move_up(zz):
        return (UP, COLUMN, column(zz), device(z + 1, x, c, y))

    def move_down(zz):
        return (DOWN, COLUMN, column(zz), device(z - 1, x, c, y))

    def first_up(zz):
        return (UP_FIRST, FIRST, of_first(zz), device(z + 1, x, c, y))

    def first_down(zz):
        return (DOWN_FIRST, FIRST, of_first(zz), device(z - 1, x, c, y))

    def along(zz, rising, falling, up, down):
        if rising:

            @pl.when(z < nz - 1)
            def _():
                start(*up(zz))

        if falling:

            @pl.when(z > 0)
            def _():
                start(*down(zz))

    def stage0(zz, rising, falling, wait):
        if wait:
            arrived(UP, COLUMN, column(zz), to_core)
        if z_second and not wait:
            start(FIRST, FIRST, column(zz), to_first)
        along(zz, rising, falling, move_up, move_down)
        if not z_second:
            start(FIRST, FIRST, column(zz), to_first)
        start(SECOND, SECOND, column(zz), to_second)
        start(CORE, CORE, column(zz), to_core)

    def stage1(zz, rising, falling):
        arrived(FIRST, FIRST, of_first(zz), to_first)
        if z_second:
            along(zz, rising, falling, first_up, first_down)
        start(BOTH, BOTH, of_first(zz), to_second)
        start(core_first, core_first, of_first(zz), to_core)

    def stage2(zz, rising, falling):
        arrived(SECOND, SECOND, of_second(zz), to_second)
        start(core_second, core_second, of_second(zz), to_core)
        arrived(BOTH, BOTH, of_both(zz), to_second)
        start(CORE + 3, CORE + 3, of_both(zz), to_core)

    def begin():
        stage0(z, True, True, False)

    def step(t):
        @pl.when((t < nz) & (z - t >= 0))
        def _():
            stage0(z - t, True, False, True)

        @pl.when((t < nz) & (z + t < nz))
        def _():
            stage0(z + t, False, True, True)

        for lag, stage in ((1, stage1), (2, stage2)):
            late = t - lag

            @pl.when(late == 0)
            def _():
                stage(z, True, True)

            @pl.when((late > 0) & (late < nz) & (z - late >= 0))
            def _():
                stage(z - late, True, False)

            @pl.when((late > 0) & (late < nz) & (z + late < nz))
            def _():
                stage(z + late, False, True)

    def all_arrived(zz, carry):
        for fx in range(2):
            for fy in range(2):
                kind = CORE + 2 * fx + fy
                shard = (zz, x + fx * (1 - 2 * x), 1 - c, y + fy * (1 - 2 * y))
                arrived(kind, kind, shard, to_core)
        return carry

    def all_sent(zz, carry):
        @pl.when((zz <= z) & (z < nz - 1))
        def _():
            sent(*move_up(zz))

        @pl.when((zz >= z) & (z > 0))
        def _():
            sent(*move_down(zz))

        if z_second:

            @pl.when((zz <= z) & (z < nz - 1))
            def _():
                sent(*first_up(zz))

            @pl.when((zz >= z) & (z > 0))
            def _():
                sent(*first_down(zz))

            @pl.when(zz == z)
            def _():
                sent(FIRST, FIRST, column(zz), to_first)

        else:
            sent(FIRST, FIRST, column(zz), to_first)
        sent(SECOND, SECOND, column(zz), to_second)
        sent(BOTH, BOTH, of_first(zz), to_second)
        sent(CORE, CORE, column(zz), to_core)
        sent(core_first, core_first, of_first(zz), to_core)
        sent(core_second, core_second, of_second(zz), to_core)
        sent(CORE + 3, CORE + 3, of_both(zz), to_core)
        return carry

    def end_arrive():
        lax.fori_loop(0, nz, all_arrived, 0)

    def end_send():
        lax.fori_loop(0, nz, all_sent, 0)

    return begin, step, end_arrive, end_send


def swap_halves(place, rows, other, sem):
    z, x, c, y = place
    return remote(
        rows.at[pl.ds(LOCAL * (1 - y), LOCAL)],
        other,
        sem.at[0],
        sem.at[1],
        device(z, x, c, 1 - y),
    )


def gather_kernel(nz, views, *refs):
    n = len(views)
    srcs, tokens, outs, other = refs[:n], refs[n], refs[n + 1 : 2 * n + 1], refs[2 * n + 1]
    send_sem, recv_sem, own_sem, swap_sem = refs[2 * n + 2 :]
    place = my_place()
    halves = swap_halves(place, tokens, other, swap_sem)
    own = [
        pltpu.make_async_copy(src, view(out, *place), own_sem.at[i])
        for i, (src, out, view) in enumerate(zip(srcs, outs, views))
    ]
    for copy in own:
        copy.start()
    entry_barrier(nz)
    halves.start()
    for copy in own:
        copy.wait()
    pieces = [(i, out, view) for i, (out, view) in enumerate(zip(outs, views))]
    begin, step, end_arrive, end_send = gather_steps(
        nz, place, place[2], False, pieces, send_sem, recv_sem
    )
    begin()

    def loop(t, carry):
        step(t)
        return carry

    lax.fori_loop(1, nz + 2, loop, 0)
    end_send()
    end_arrive()
    halves.wait()


def gather(nz, collective_id, parts, tokens):
    shards, shapes, views = zip(*parts)
    n = len(parts)
    return pl.pallas_call(
        functools.partial(gather_kernel, nz, views),
        in_specs=[ANY] * (n + 1),
        out_specs=[ANY] * (n + 1),
        out_shape=[sds(shape, shard.dtype) for shard, shape in zip(shards, shapes)]
        + [sds((LOCAL, *tokens.shape[1:]), tokens.dtype)],
        scratch_shapes=[
            pltpu.SemaphoreType.DMA((11, nz, n)),
            pltpu.SemaphoreType.DMA((8, nz, n)),
            pltpu.SemaphoreType.DMA((n,)),
            pltpu.SemaphoreType.DMA((2,)),
        ],
        name="gather",
        compiler_params=params(collective_id=collective_id, has_side_effects=True),
    )(*shards, tokens)


def scatter_kernel(nz, views, *refs):
    n = len(views)
    terms, outs = refs[:n], refs[n : 2 * n]
    mine, from_core, from_second, from_first, from_below, from_above = (
        refs[2 * n + i * n : 3 * n + i * n] for i in range(6)
    )
    send_sem, recv_sem, own_sem = refs[8 * n :]
    place = z, x, c, y = my_place()
    first, second, both = partners(place, place[2])
    to_first = device(z, first[0], c, first[1])
    to_second = device(z, second[0], c, second[1])
    to_core = device(z, x, 1 - c, y)

    def copies(srcs, dsts, send, recv, zz, target):
        return [
            pltpu.make_async_remote_copy(
                src_ref=srcs[i],
                dst_ref=dsts[i],
                send_sem=send_sem.at[send, zz, i],
                recv_sem=recv_sem.at[recv, zz, i],
                device_id=target,
                device_id_type=pl.DeviceIdType.MESH,
            )
            for i in range(n)
        ]

    def slots(bufs, *index):
        return [b.at[index] for b in bufs]

    def pick(refs_, *index):
        return [b[index] for b in refs_]

    flips = [(fx, fy) for fx in range(2) for fy in range(2)]

    def at(fx, fy):
        return x + fx * (1 - 2 * x), y + fy * (1 - 2 * y)

    def core_copies(zz, f):
        fx, fy = flips[f]
        xx, yy = at(fx, fy)
        return copies(
            [view(t, zz, xx, 1 - c, yy) for t, view in zip(terms, views)],
            slots(from_core, zz, f),
            f,
            f,
            zz,
            to_core,
        )

    def own_copies(zz, f):
        fx, fy = flips[f]
        xx, yy = at(fx, fy)
        return [
            pltpu.make_async_copy(
                view(t, zz, xx, c, yy), mine[i].at[zz, f], own_sem.at[f, zz, i]
            )
            for i, (t, view) in enumerate(zip(terms, views))
        ]

    f_first, f_second = 2 - c, 1 + c

    def second_copies(zz, across):
        return copies(
            slots(from_core, zz, 3 if across else f_second),
            slots(from_second, zz, 1 if across else 0),
            4 + across,
            4 + across,
            zz,
            to_second,
        )

    def first_copies(zz):
        return copies(slots(from_second, zz, 1), slots(from_first, zz), 6, 6, zz, to_first)

    def up_copies(zz):
        return copies(slots(from_first, zz), slots(from_below, zz), 7, 7, zz, device(z + 1, x, c, y))

    def down_copies(zz):
        return copies(slots(from_first, zz), slots(from_above, zz), 8, 8, zz, device(z - 1, x, c, y))

    def run(group, what):
        for copy in group:
            getattr(copy, what)()

    def add(into, index, other, other_index):
        for i in range(n):
            a, b = into[i].at[index], other[i].at[other_index]
            a[...] = (a[...].astype(F32) + b[...].astype(F32)).astype(a.dtype)

    def by_distance(t, do):
        @pl.when((t >= 0) & (t < nz) & (z - t >= 0))
        def _():
            do(z - t)

        @pl.when((t > 0) & (t < nz) & (z + t < nz))
        def _():
            do(z + t)

    def start_own(zz):
        for f in range(4):
            run(own_copies(zz, f), "start")

    def start_core(zz):
        for f in (3, 1, 2, 0):
            run(core_copies(zz, f), "start")

    def stage0(zz):
        for f in (3, 1, 2, 0):
            run(core_copies(zz, f), "wait_recv")
            run(own_copies(zz, f), "wait")
            add(from_core, (zz, f), mine, (zz, f))
        run(second_copies(zz, 1), "start")
        run(second_copies(zz, 0), "start")

    def stage1(zz):
        run(second_copies(zz, 1), "wait_recv")
        add(from_second, (zz, 1), from_core, (zz, f_first))
        run(first_copies(zz), "start")

    def stage2(zz):
        run(second_copies(zz, 0), "wait_recv")
        add(from_second, (zz, 0), from_core, (zz, 0))
        run(first_copies(zz), "wait_recv")
        add(from_first, (zz,), from_second, (zz, 0))

        @pl.when(zz > z)
        def _():
            @pl.when(z > 0)
            def _():
                run(up_copies(zz), "wait_recv")
                add(from_first, (zz,), from_below, (zz,))

            run(up_copies(zz), "start")

        @pl.when(zz < z)
        def _():
            @pl.when(z < nz - 1)
            def _():
                run(down_copies(zz), "wait_recv")
                add(from_first, (zz,), from_above, (zz,))

            run(down_copies(zz), "start")

    entry_barrier(nz)

    def begin(k, carry):
        by_distance(nz - 1 - k, start_core)
        by_distance(nz - 1 - k, start_own)
        return carry

    lax.fori_loop(0, nz, begin, 0)

    def step(k, carry):
        t = nz - 1 - k
        by_distance(t, stage0)
        by_distance(t + 1, stage1)
        by_distance(t + 2, stage2)
        return carry

    lax.fori_loop(0, nz + 2, step, 0)

    @pl.when(z > 0)
    def _():
        run(up_copies(z), "wait_recv")
        add(from_first, (z,), from_below, (z,))

    @pl.when(z < nz - 1)
    def _():
        run(down_copies(z), "wait_recv")
        add(from_first, (z,), from_above, (z,))

    for i in range(n):
        outs[i][...] = from_first[i][z]

    def finish(zz, carry):
        for f in range(4):
            run(core_copies(zz, f), "wait_send")
        run(second_copies(zz, 1), "wait_send")
        run(second_copies(zz, 0), "wait_send")
        run(first_copies(zz), "wait_send")

        @pl.when(zz > z)
        def _():
            run(up_copies(zz), "wait_send")

        @pl.when(zz < z)
        def _():
            run(down_copies(zz), "wait_send")

        return carry

    lax.fori_loop(0, nz, finish, 0)


def scatter(nz, collective_id, parts):
    terms, shapes, views = zip(*parts)
    n = len(parts)
    dtypes = [t.dtype for t in terms]

    def bufs(*lead):
        return [pltpu.VMEM((*lead, *shape), d) for shape, d in zip(shapes, dtypes)]

    return pl.pallas_call(
        functools.partial(scatter_kernel, nz, views),
        in_specs=[ANY] * n,
        out_specs=[VMEM] * n,
        out_shape=[sds(shape, d) for shape, d in zip(shapes, dtypes)],
        scratch_shapes=[
            *bufs(nz, 4),
            *bufs(nz, 4),
            *bufs(nz, 2),
            *bufs(nz),
            *bufs(nz),
            *bufs(nz),
            pltpu.SemaphoreType.DMA((9, nz, n)),
            pltpu.SemaphoreType.DMA((9, nz, n)),
            pltpu.SemaphoreType.DMA((4, nz, n)),
        ],
        name="scatter",
        compiler_params=params(62, collective_id=collective_id, has_side_effects=True),
    )(*terms)


def whole_rows(side, mine, other):
    mine, other = mine.astype(F32), other.astype(F32)
    first = jnp.where(side == 0, mine, other)
    second = jnp.where(side == 0, other, mine)
    return jnp.concatenate([jnp.zeros((MEM, D), F32), first, second], axis=0)


def split_rows(side, rows):
    half = (SEG - MEM) // 2
    first, second = rows[MEM : MEM + half], rows[MEM + half :]
    keep = jnp.where(side == 0, first, second)
    send = jnp.where(side == 0, second, first)
    return keep, send


def project_kernel(mine_ref, other_ref, w_ref, table_ref, x_ref, q_ref, k_ref, v_ref):
    side = lax.axis_index("tensor")
    mine = mine_ref[LOCAL * side + pl.program_id(0)]
    x = whole_rows(side, mine, other_ref[0]).astype(BF16)
    x_ref[0] = x
    query = nn(x, w_ref[0]) + table_ref[QUERY_BIAS : QUERY_BIAS + 1, :]
    q_ref[0] = (query * SCALE).astype(BF16)
    k_ref[0] = nn(x, w_ref[1]).astype(BF16)
    v_ref[0] = (nn(x, w_ref[2]) + table_ref[VALUE_BIAS : VALUE_BIAS + 1, :]).astype(BF16)


def slot_rows(width=D):
    return pl.BlockSpec((1, SEG, width), lambda s: (s, 0, 0))


def half_rows(half):
    return pl.BlockSpec((1, half, D), lambda s: (s, 0, 0))


def project(tokens, other, attn, table):
    return pl.pallas_call(
        project_kernel,
        grid=(LOCAL,),
        in_specs=[
            once(tokens.shape, (0, 0, 0)),
            half_rows(tokens.shape[1]),
            once((3, D, D), (0, 0, 0)),
            once((NVEC, D), (0, 0)),
        ],
        out_specs=[slot_rows()] * 4,
        out_shape=[sds((LOCAL, SEG, D), BF16)] * 4,
        name="project",
        compiler_params=params(),
    )(tokens, other, attn, table)


def head_masks():
    feature_head = lax.broadcasted_iota(jnp.int32, (1, D), 1) // DH
    return [feature_head == h for h in range(HEADS)]


def by_head(rows16, masks):
    zero = jnp.zeros_like(rows16)
    return jnp.concatenate([jnp.where(m, rows16, zero) for m in masks], axis=0)


def own_columns(blocks, masks):
    total = jnp.zeros((THIN, D), blocks.dtype)
    for h, m in enumerate(masks):
        total = jnp.where(m, blocks[THIN * h : THIN * (h + 1)], total)
    return total


def copies_of(key_mask_shape):
    row = lax.rem(lax.broadcasted_iota(jnp.int32, key_mask_shape, 0), THIN)
    key = lax.broadcasted_iota(jnp.int32, key_mask_shape, 1)
    return jnp.where((key < MEM) & (key <= row), 2.0, 1.0)


def pair_barrier(place):
    z, x, c, y = place
    barrier = pltpu.get_barrier_semaphore()
    pl.semaphore_signal(
        barrier,
        inc=1,
        device_id=device(z, x, c, 1 - y),
        device_id_type=pl.DeviceIdType.MESH,
    )
    pl.semaphore_wait(barrier, 1)


def chain_kernel(
    place_ref,
    table_ref,
    attn_ref,
    ffn_ref,
    x_in,
    q_in,
    k_in,
    v_in,
    cot_ref,
    x_ref,
    q_ref,
    k_ref,
    v_ref,
    saved_d_ref,
    saved_f_ref,
    saved_s_ref,
    cot_other_ref,
    wa,
    wf,
    xb,
    qb,
    kb,
    vb,
    save_d,
    save_f,
    save_s,
    left,
    given,
    sem_w,
    sem_x,
    sem_kv,
    sem_out,
    sem_memory,
    sem_cot,
):
    del x_in, q_in, k_in, v_in
    place = z, x, c, y = my_place()
    loads = [
        pltpu.make_async_copy(attn_ref, wa, sem_w.at[0]),
        pltpu.make_async_copy(ffn_ref.at[0], wf.at[0], sem_w.at[1]),
        pltpu.make_async_copy(ffn_ref.at[1], wf.at[1], sem_w.at[2]),
    ]
    tiles = [
        pltpu.make_async_copy(x_ref.at[s, pl.ds(0, THIN)], xb.at[s], sem_x.at[s])
        for s in range(LOCAL)
    ]
    keys = [
        pltpu.make_async_copy(src.at[s], dst.at[s], sem_kv.at[2 * s + i])
        for s in range(LOCAL)
        for i, (src, dst) in enumerate(((k_ref, kb), (v_ref, vb)))
    ]
    for copy in tiles + loads[:1] + keys + loads[1:]:
        copy.start()
    pair_barrier(place)
    cot_swap = swap_halves(place, cot_ref, cot_other_ref, sem_cot)
    cot_swap.start()
    handed = remote(left, given, sem_memory.at[0], sem_memory.at[1], device(z, x, c, 1 - y))

    masks = head_masks()
    memory_row = lax.broadcasted_iota(jnp.int32, (THIN, 1), 0) < MEM
    first = table_ref[FIRST_MEMORY:NVEC, :]
    first = jnp.concatenate([first, jnp.zeros((THIN - MEM, D), F32)], axis=0)
    row = lambda r: table_ref[r : r + 1, :]

    def slots(turn, memory):
        for s in range(LOCAL):
            tiles[s].wait()
            if s == 0:
                loads[0].wait()
            keys[2 * s].wait()
            keys[2 * s + 1].wait()
            if memory is None:
                memory = first
            else:
                memory = jnp.where(place_ref[LOCAL * turn + s] == 0, first, memory)
            x16 = jnp.where(memory_row, memory, xb[s].astype(F32)).astype(BF16)
            xb[s] = x16
            qb[s] = ((nn(x16, wa[0]) + row(QUERY_BIAS)) * SCALE).astype(BF16)
            kb[s, 0:THIN] = nn(x16, wa[1]).astype(BF16)
            vb[s, 0:THIN] = (nn(x16, wa[2]) + row(VALUE_BIAS)).astype(BF16)
            outs = [
                pltpu.make_async_copy(
                    src.at[s, pl.ds(0, THIN)], dst.at[s, pl.ds(0, THIN)], sem_out.at[4 * s + i]
                )
                for i, (src, dst) in enumerate(
                    ((xb, x_ref), (qb, q_ref), (kb, k_ref), (vb, v_ref))
                )
            ]
            for copy in outs:
                copy.start()
            if turn == 1 and s == LOCAL - 1:
                save_d[s] = jnp.zeros_like(save_d[s])
                save_f[s] = jnp.zeros_like(save_f[s])
                save_s[s] = jnp.zeros_like(save_s[s])
            else:
                q_heads = by_head(qb[s], masks)
                score = nt(q_heads, kb[s])
                top = jnp.max(score, axis=-1, keepdims=True)
                weight = jnp.exp(score - top) * copies_of(score.shape)
                total = jnp.sum(weight, axis=-1, keepdims=True)
                share = (weight / total).astype(BF16)
                log_total = top + jnp.log(total)
                context = own_columns(nn(share, vb[s]), masks).astype(BF16)
                unit1, inverse1 = normalized(
                    x16.astype(F32) + nt(context, wa[3]) + row(OUT_BIAS)
                )
                hidden = (unit1 * row(GAIN1) + row(SHIFT1)).astype(BF16)
                if s == 0:
                    loads[1].wait()
                up = nt(hidden, wf[0])
                up_bias = jnp.concatenate([row(UP_BIAS + i) for i in range(FF // D)], axis=1)
                active16, slope = gelu_parts(up + up_bias)
                active16 = active16.astype(BF16)
                if s == 0:
                    loads[2].wait()
                second = hidden.astype(F32) + nn(active16, wf[1]) + row(DOWN_BIAS)
                unit2, inverse2 = normalized(second)
                output = (unit2 * row(GAIN2) + row(SHIFT2)).astype(BF16)
                memory = output.astype(F32)
                if turn == 0 and s == LOCAL - 1:
                    left[...] = output
                    handed.start()
                save_d[s, 0] = hidden
                save_d[s, 1] = unit1.astype(BF16)
                save_d[s, 2] = unit2.astype(BF16)
                save_d[s, 3] = context
                save_f[s, 0] = active16
                save_f[s, 1] = slope.astype(BF16)
                wide = lambda v: jnp.broadcast_to(v, (v.shape[0], 128))
                save_s[s, 0 : HEADS * THIN] = wide(log_total)
                save_s[s, HEADS * THIN : HEADS * THIN + THIN] = wide(inverse1)
                save_s[s, HEADS * THIN + THIN :] = wide(inverse2)
            for copy in outs:
                copy.wait()

    @pl.when(y == 0)
    def _():
        slots(0, None)
        handed.wait_send()

    @pl.when(y == 1)
    def _():
        handed.wait_recv()
        slots(1, given[...].astype(F32))

    saves = [
        pltpu.make_async_copy(save_d, saved_d_ref, sem_out.at[0]),
        pltpu.make_async_copy(save_f, saved_f_ref, sem_out.at[1]),
        pltpu.make_async_copy(save_s, saved_s_ref, sem_out.at[2]),
    ]
    for copy in saves:
        copy.start()
    for copy in saves:
        copy.wait()
    cot_swap.wait()


SAVED = (
    sds((LOCAL, 4, THIN, D), BF16),
    sds((LOCAL, 2, THIN, FF), BF16),
    sds((LOCAL, HEADS * THIN + 2 * THIN, 128), F32),
)


def chain(place, table, attn, ffn, x, q, k, v, cot):
    whole = sds((LOCAL, SEG, D), BF16)
    outs = pl.pallas_call(
        chain_kernel,
        in_specs=[SMEM, VMEM] + [ANY] * 7,
        out_specs=[ANY] * 8,
        out_shape=[whole] * 4 + list(SAVED) + [sds((LOCAL, *cot.shape[1:]), BF16)],
        input_output_aliases={4 + i: i for i in range(4)},
        scratch_shapes=[
            pltpu.VMEM((4, D, D), BF16),
            pltpu.VMEM((2, FF, D), BF16),
            pltpu.VMEM((LOCAL, THIN, D), BF16),
            pltpu.VMEM((LOCAL, THIN, D), BF16),
            pltpu.VMEM((LOCAL, SEG, D), BF16),
            pltpu.VMEM((LOCAL, SEG, D), BF16),
            *[pltpu.VMEM(s.shape, s.dtype) for s in SAVED],
            pltpu.VMEM((THIN, D), BF16),
            pltpu.VMEM((THIN, D), BF16),
            pltpu.SemaphoreType.DMA((3,)),
            pltpu.SemaphoreType.DMA((LOCAL,)),
            pltpu.SemaphoreType.DMA((2 * LOCAL,)),
            pltpu.SemaphoreType.DMA((4 * LOCAL,)),
            pltpu.SemaphoreType.DMA((2,)),
            pltpu.SemaphoreType.DMA((2,)),
        ],
        name="chain",
        compiler_params=params(collective_id=2, has_side_effects=True),
    )(place, table, attn, ffn, x, q, k, v, cot)
    return outs[:4], outs[4:7], outs[7]


def own_lanes(block, head):
    lane = lax.broadcasted_iota(jnp.int32, block.shape, 1)
    return jnp.where((lane < DH) == (head == 0), block, jnp.zeros_like(block))


def seen(score, first_query):
    key = lax.broadcasted_iota(jnp.int32, score.shape, 0)
    query = lax.broadcasted_iota(jnp.int32, score.shape, 1) + first_query
    return key <= query


def attend_pair(q, k, v):
    contexts_of, logs_of = [], [[], []]
    for part in range(SEG // TILE):
        rows = slice(TILE * part, TILE * (part + 1))
        keys = slice(0, TILE * (part + 1))
        contexts = []
        for head in range(2):
            score = nt(own_lanes(k[keys], head), q[rows])
            key = lax.broadcasted_iota(jnp.int32, score.shape, 0)
            allowed = seen(score, TILE * part) & (key >= MEM)
            score = jnp.where(allowed, score, MASK_VALUE)
            top = jnp.max(score, axis=0, keepdims=True)
            weight = jnp.exp(score - top)
            total = jnp.sum(weight, axis=0, keepdims=True)
            share = (weight * (1.0 / total)).astype(BF16)
            logs_of[head].append(top + jnp.log(total))
            contexts.append(tn(share, v[keys]))
        lane = lax.broadcasted_iota(jnp.int32, contexts[0].shape, 1)
        contexts_of.append(jnp.where(lane < DH, contexts[0], contexts[1]).astype(BF16))
    return jnp.concatenate(contexts_of, axis=0), [jnp.concatenate(l, axis=1) for l in logs_of]


def attend_kernel(q_ref, k_ref, v_ref, c_ref, log_ref):
    context, logs = attend_pair(q_ref[0], k_ref[0], v_ref[0])
    c_ref[0] = context
    for head in range(2):
        log_ref[0, 0, head : head + 1] = logs[head]


def with_memory(q, k16, v16, context, log_tokens):
    masks = head_masks()
    score = nt(by_head(k16, masks), q).reshape(HEADS, THIN, SEG)
    key = lax.broadcasted_iota(jnp.int32, score.shape, 1)
    score = jnp.where(key < MEM, score, MASK_VALUE)
    top = jnp.maximum(jnp.max(score, axis=1), log_tokens)
    weight = jnp.exp(score - top[:, None])
    old = jnp.exp(log_tokens - top)
    total = jnp.sum(weight, axis=1) + old
    share = (weight * (1.0 / total)[:, None]).reshape(HEADS * THIN, SEG).astype(BF16)
    kept = old / total
    coarse = kept.astype(BF16)
    fine = (kept - coarse.astype(F32)).astype(BF16)
    pad = jnp.zeros((4, SEG), BF16)
    head = lax.rem(lax.broadcasted_iota(jnp.int32, (2 * THIN, D), 0), THIN)
    spread = jnp.where(head == lax.broadcasted_iota(jnp.int32, (2 * THIN, D), 1) // DH, 1.0, 0.0)
    factor = tn(jnp.concatenate([coarse, pad, fine, pad], axis=0), spread.astype(BF16))
    context = factor * context.astype(F32) + tn(share, by_head(v16, masks))
    return context.astype(BF16), top + jnp.log(total)


PAIR = pl.BlockSpec((1, SEG, 2 * DH), lambda s, h: (s, 0, h))
PAIR_LOG = pl.BlockSpec((1, 1, 2, SEG), lambda s, h: (s, h, 0, 0))


def attend(q, k, v):
    return pl.pallas_call(
        attend_kernel,
        grid=(LOCAL, HEADS // 2),
        in_specs=[PAIR] * 3,
        out_specs=[PAIR, PAIR_LOG],
        out_shape=[sds((LOCAL, SEG, D), BF16), sds((LOCAL, HEADS // 2, 2, SEG), F32)],
        name="attend",
        compiler_params=params(),
    )(q, k, v)


def attend_back_kernel(q_ref, k_ref, v_ref, dc_ref, log_ref, dq_ref, dk_ref, dv_ref):
    last = SEG // TILE
    key_terms, value_terms = [], []
    for head in range(2):
        key_sum, value_sum = [], []
        query_parts = []
        for part in range(last):
            rows = slice(TILE * part, TILE * (part + 1))
            keys = slice(0, TILE * (part + 1))
            q, dc = q_ref[0, rows], dc_ref[0, rows]
            k = k_ref[0, keys]
            score = nt(own_lanes(k, head), q)
            share = jnp.exp(score - log_ref[0, 0, head : head + 1, rows])
            share = jnp.where(seen(score, TILE * part), share, 0.0)
            share_grad = nt(own_lanes(v_ref[0, keys], head), dc)
            inner = jnp.sum(share_grad * share, axis=0, keepdims=True)
            score_grad = (share * (share_grad - inner)).astype(BF16)
            value_sum.append(nn(share.astype(BF16), dc))
            key_sum.append(nn(score_grad, q))
            query_parts.append(tn(score_grad, k))
        key_terms.append(key_sum)
        value_terms.append(value_sum)
        if head == 0:
            first_queries = query_parts
    for part in range(last):
        rows = slice(TILE * part, TILE * (part + 1))
        lane = lax.broadcasted_iota(jnp.int32, (TILE, 2 * DH), 1)
        pick = lambda a, b: jnp.where(lane < DH, a, b)
        dq_ref[0, rows] = (pick(first_queries[part], query_parts[part]) * SCALE).astype(BF16)
        for terms, out in ((key_terms, dk_ref), (value_terms, dv_ref)):
            total = None
            for later in range(part, last):
                term = pick(terms[0][later][rows], terms[1][later][rows])
                total = term if total is None else total + term
            out[0, rows] = total.astype(BF16)


def attend_back(q, k, v, dc, log_total):
    return pl.pallas_call(
        attend_back_kernel,
        grid=(LOCAL, HEADS // 2),
        in_specs=[PAIR] * 4 + [PAIR_LOG],
        out_specs=[PAIR] * 3,
        out_shape=[sds((LOCAL, SEG, D), BF16)] * 3,
        name="attend_back",
        compiler_params=params(),
    )(q, k, v, dc, log_total)


def rows_kernel(
    place_ref,
    x_ref,
    q_ref,
    k16_ref,
    v16_ref,
    tokens_c_ref,
    tokens_log_ref,
    mine_ref,
    other_ref,
    wo_ref,
    wf_ref,
    table_ref,
    keep_ref,
    send_ref,
    h_ref,
    g_ref,
    du_ref,
    df_ref,
    da_ref,
    dc_ref,
    c_ref,
    log_ref,
    sums_ref,
    slope_ref,
):
    row = lambda r: table_ref[r : r + 1, :]
    slot = pl.program_id(0)
    side = lax.axis_index("tensor")
    live = place_ref[LOCAL * side + slot] >= 0

    @pl.when(slot == 0)
    def _():
        sums_ref[...] = jnp.zeros_like(sums_ref)

    def add(r, value):
        sums_ref[r : r + 1, :] += value

    log_tokens = jnp.concatenate([tokens_log_ref[0, h] for h in range(HEADS // 2)], axis=0)
    context, log_total = with_memory(
        q_ref[0], k16_ref[0], v16_ref[0], tokens_c_ref[0], log_tokens
    )
    c_ref[0] = context
    for h in range(HEADS // 2):
        log_ref[0, h] = log_total[2 * h : 2 * h + 2]
    unit1, inverse1 = normalized(x_ref[0].astype(F32) + nt(context, wo_ref[0]) + row(OUT_BIAS))
    hidden = (unit1 * row(GAIN1) + row(SHIFT1)).astype(BF16)
    h_ref[0] = hidden
    second = hidden.astype(F32) + row(DOWN_BIAS)
    for i in range(FF // D):
        cols = slice(D * i, D * (i + 1))
        up = nt(hidden, wf_ref[0, cols]) + row(UP_BIAS + i)
        active, slope = gelu_parts(up)
        active = active.astype(BF16)
        g_ref[0, :, cols] = active
        slope_ref[:, cols] = slope.astype(BF16)
        second = second + nn(active, wf_ref[1, cols])
    unit2, inverse2 = normalized(second)
    output = jnp.where(live, unit2 * row(GAIN2) + row(SHIFT2), 0.0)
    keep, send = split_rows(side, output)
    keep_ref[0] = keep.astype(BF16)
    send_ref[0] = send.astype(BF16)

    grad = whole_rows(side, mine_ref[LOCAL * side + slot], other_ref[0])
    grad = jnp.where(live, grad, 0.0)
    add(GAIN2, row_sum(grad * unit2))
    add(SHIFT2, row_sum(grad))
    second_grad = normalized_back(grad * row(GAIN2), unit2, inverse2)
    down_grad = second_grad.astype(BF16)
    df_ref[0] = down_grad
    add(DOWN_BIAS, row_sum(down_grad.astype(F32)))
    hidden_grad = second_grad
    for i in range(FF // D):
        cols = slice(D * i, D * (i + 1))
        up_grad = (nt(down_grad, wf_ref[1, cols]) * slope_ref[:, cols].astype(F32)).astype(BF16)
        du_ref[0, :, cols] = up_grad
        add(UP_BIAS + i, row_sum(up_grad.astype(F32)))
        hidden_grad = hidden_grad + nn(up_grad, wf_ref[0, cols])
    add(GAIN1, row_sum(hidden_grad * unit1))
    add(SHIFT1, row_sum(hidden_grad))
    branch_grad = normalized_back(hidden_grad * row(GAIN1), unit1, inverse1).astype(BF16)
    da_ref[0] = branch_grad
    add(OUT_BIAS, row_sum(branch_grad.astype(F32)))
    dc_ref[0] = nn(branch_grad, wo_ref[0]).astype(BF16)


def rows_part(place, x, q, k, v, c, log_tokens, cot, other, attn, ffn, table):
    half = cot.shape[1]
    whole, whole_wide = sds((LOCAL, SEG, D), BF16), sds((LOCAL, SEG, FF), BF16)
    part, logs = sds((LOCAL, half, D), BF16), sds((LOCAL, HEADS // 2, 2, SEG), F32)
    rows, wide = slot_rows(), slot_rows(FF)
    thin = pl.BlockSpec((1, THIN, D), lambda s: (s, 0, 0))
    log_rows = pl.BlockSpec((1, HEADS // 2, 2, SEG), lambda s: (s, 0, 0, 0))
    return pl.pallas_call(
        rows_kernel,
        grid=(LOCAL,),
        in_specs=[SMEM, rows, rows, thin, thin, rows, log_rows]
        + [once(cot.shape, (0, 0, 0)), half_rows(half)]
        + [once((1, D, D), (3, 0, 0)), once((2, FF, D), (0, 0, 0)), once((NVEC, D), (0, 0))],
        out_specs=[half_rows(half)] * 2
        + [rows, wide, wide, rows, rows, rows, rows, log_rows, once((THIN, D), (0, 0))],
        out_shape=[part] * 2
        + [whole, whole_wide, whole_wide, whole, whole, whole, whole, logs, sds((THIN, D), F32)],
        scratch_shapes=[pltpu.VMEM((SEG, FF), BF16)],
        name="rows_part",
        compiler_params=params(),
    )(place, x, q, k, v, c, log_tokens, cot, other, attn, ffn, table)


CHUNK = 768


def chain_back_kernel(
    place_ref,
    table_ref,
    attn_ref,
    ffn_ref,
    q_ref,
    k_ref,
    v_ref,
    saved_d_ref,
    saved_f_ref,
    saved_s_ref,
    g_ref,
    du_ref,
    df_ref,
    h_ref,
    send_ref,
    dk_in,
    dv_in,
    da_in,
    dq_in,
    c_in,
    dk_ref,
    dv_ref,
    da_ref,
    dq_ref,
    c_ref,
    thin_d_ref,
    thin_f_ref,
    sums_ref,
    terms_ref,
    received_ref,
    wa,
    wf,
    qb,
    kb,
    vb,
    dkb,
    dvb,
    tiles,
    df,
    hid,
    gb,
    dub,
    staged,
    save_d,
    save_f,
    save_s,
    thin_d,
    thin_f,
    sums,
    left,
    given,
    sem_w,
    sem_in,
    sem_ff,
    sem_chunk,
    sem_out,
    sem_stage,
    sem_grad,
    sem_swap,
):
    del dk_in, dv_in, da_in, dq_in, c_in
    place = z, x, c, y = my_place()
    loads = [
        pltpu.make_async_copy(attn_ref, wa, sem_w.at[0]),
        pltpu.make_async_copy(ffn_ref.at[0], wf.at[0], sem_w.at[1]),
        pltpu.make_async_copy(ffn_ref.at[1], wf.at[1], sem_w.at[2]),
    ]
    first_rows = lambda ref: ref.at[:, pl.ds(0, THIN)]
    grads = [
        pltpu.make_async_copy(dk_ref, dkb, sem_in.at[0]),
        pltpu.make_async_copy(dv_ref, dvb, sem_in.at[1]),
    ]
    saved = [
        pltpu.make_async_copy(saved_d_ref, save_d, sem_in.at[2]),
        pltpu.make_async_copy(saved_f_ref, save_f, sem_in.at[3]),
        pltpu.make_async_copy(saved_s_ref, save_s, sem_in.at[4]),
    ]
    reads = [
        pltpu.make_async_copy(first_rows(q_ref), qb, sem_in.at[5]),
        pltpu.make_async_copy(k_ref, kb, sem_in.at[6]),
        pltpu.make_async_copy(v_ref, vb, sem_in.at[7]),
    ]
    merged = (da_ref, dq_ref, c_ref)
    tile_reads = [
        pltpu.make_async_copy(first_rows(ref), tiles.at[i], sem_in.at[8 + i])
        for i, ref in enumerate(merged)
    ]
    rows_in = [
        pltpu.make_async_copy(df_ref, df, sem_ff.at[0]),
        pltpu.make_async_copy(h_ref, hid, sem_ff.at[1]),
    ]

    def chunk_reads(i):
        lanes = pl.ds(CHUNK * i, CHUNK)
        return [
            pltpu.make_async_copy(src.at[:, :, lanes], dst.at[i % 2], sem_chunk.at[i % 2, j])
            for j, (src, dst) in enumerate(((g_ref, gb), (du_ref, dub)))
        ]

    @pl.when(y == 1)
    def _():
        for copy in grads + loads[:1] + saved + loads[:0:-1] + reads + tile_reads:
            copy.start()
        for copy in rows_in + chunk_reads(0) + chunk_reads(1):
            copy.start()

    @pl.when(y == 0)
    def _():
        for copy in rows_in + chunk_reads(0) + chunk_reads(1):
            copy.start()
        for copy in grads + loads[:1] + saved + loads[:0:-1] + reads + tile_reads:
            copy.start()

    pair_barrier(place)
    swap = remote(
        send_ref, received_ref, sem_swap.at[0], sem_swap.at[1], device(z, x, c, 1 - y)
    )
    swap.start()
    handed = remote(left, given, sem_grad.at[0], sem_grad.at[1], device(z, x, c, 1 - y))

    sums[...] = jnp.zeros_like(sums)
    thin_d[...] = jnp.zeros_like(thin_d)
    thin_f[...] = jnp.zeros_like(thin_f)
    masks = head_masks()
    memory_row = lax.broadcasted_iota(jnp.int32, (THIN, 1), 0) < MEM
    row = lambda r: table_ref[r : r + 1, :]

    def add(r, value):
        sums[r : r + 1, :] += value

    def slots(turn, grad):
        waited = set()

        def need(*copies):
            for copy in copies:
                if id(copy) not in waited:
                    waited.add(id(copy))
                    copy.wait()

        for s in reversed(range(LOCAL)):
            if turn == 1 and s == LOCAL - 1:
                grad = jnp.zeros((THIN, D), F32)
            else:
                after = place_ref[LOCAL * turn + s + 1]
                grad = jnp.where(memory_row, jnp.where(after > 0, grad, 0.0), 0.0)
                need(*saved)
                unit1, unit2 = save_d[s, 1].astype(F32), save_d[s, 2].astype(F32)
                base = HEADS * THIN
                log_total = save_s[s, 0:base, 0:1]
                inverse1 = save_s[s, base : base + THIN, 0:1]
                inverse2 = save_s[s, base + THIN :, 0:1]
                add(GAIN2, row_sum(grad * unit2))
                add(SHIFT2, row_sum(grad))
                second_grad = normalized_back(grad * row(GAIN2), unit2, inverse2)
                down_grad = second_grad.astype(BF16)
                add(DOWN_BIAS, row_sum(down_grad.astype(F32)))
                need(loads[2])
                up_grad = (nt(down_grad, wf[1]) * save_f[s, 1].astype(F32)).astype(BF16)
                up_sum = row_sum(up_grad.astype(F32))
                for i in range(FF // D):
                    add(UP_BIAS + i, up_sum[:, D * i : D * (i + 1)])
                need(loads[1])
                hidden_grad = second_grad + nn(up_grad, wf[0])
                add(GAIN1, row_sum(hidden_grad * unit1))
                add(SHIFT1, row_sum(hidden_grad))
                pre_grad = normalized_back(hidden_grad * row(GAIN1), unit1, inverse1)
                branch_grad = pre_grad.astype(BF16)
                add(OUT_BIAS, row_sum(branch_grad.astype(F32)))
                need(loads[0])
                context_grad = nn(branch_grad, wa[3]).astype(BF16)
                dc_heads = by_head(context_grad, masks)
                need(*reads)
                q_heads = by_head(qb[s], masks)
                score = nt(q_heads, kb[s])
                share = jnp.exp(score - log_total) * copies_of(score.shape)
                share_grad = nt(dc_heads, vb[s])
                inner = jnp.sum(share_grad * share, axis=-1, keepdims=True)
                score_grad = (share * (share_grad - inner)).astype(BF16)
                query_grad = (own_columns(nn(score_grad, kb[s]), masks) * SCALE).astype(BF16)
                need(*grads)
                dkb[s] = (dkb[s].astype(F32) + tn(score_grad, q_heads)).astype(BF16)
                dvb[s] = (dvb[s].astype(F32) + tn(share.astype(BF16), dc_heads)).astype(BF16)
                thin_d[s, 0] = down_grad
                thin_d[s, 1] = save_d[s, 0]
                thin_f[s, 0] = up_grad
                thin_f[s, 1] = save_f[s, 0]
                need(*tile_reads)
                for i, value in enumerate((branch_grad, query_grad, save_d[s, 3])):
                    tiles[i, s] = jnp.where(memory_row, value, tiles[i, s])
                grad = pre_grad + nt(query_grad, wa[0])
            need(loads[0], *grads)
            grad = grad + nt(dkb[s, 0:THIN], wa[1]) + nt(dvb[s, 0:THIN], wa[2])
            first = jnp.where(place_ref[LOCAL * turn + s] == 0, grad, 0.0)
            sums[FIRST_MEMORY : FIRST_MEMORY + THIN, :] += first
        return grad

    @pl.when(y == 1)
    def _():
        left[...] = slots(1, None)
        handed.start()

    for copy in rows_in:
        copy.wait()
    for s in range(LOCAL):
        df[s, 0:THIN] = jnp.where(memory_row, thin_d[s, 0], df[s, 0:THIN])
        hid[s, 0:THIN] = jnp.where(memory_row, thin_d[s, 1], hid[s, 0:THIN])
    chunks = FF // CHUNK
    stores = [
        pltpu.make_async_copy(
            staged.at[i % 2], terms_ref.at[:, pl.ds(CHUNK * i, CHUNK)], sem_stage.at[i % 2]
        )
        for i in range(chunks)
    ]
    for i in range(chunks):
        for copy in chunk_reads(i):
            copy.wait()
        lanes = slice(CHUNK * i, CHUNK * (i + 1))
        for s in range(LOCAL):
            for j, buf in ((1, gb), (0, dub)):
                old = buf[i % 2, s, 0:THIN]
                buf[i % 2, s, 0:THIN] = jnp.where(memory_row, thin_f[s, j, :, lanes], old)
        if i >= 2:
            stores[i - 2].wait()
        for j, (buf, rows) in enumerate(((dub, hid), (gb, df))):
            terms = tn(
                buf[i % 2].reshape(LOCAL * SEG, CHUNK), rows[...].reshape(LOCAL * SEG, D)
            )
            staged[i % 2, j] = terms.astype(BF16)
        stores[i].start()
        if i + 2 < chunks:
            for copy in chunk_reads(i + 2):
                copy.start()

    @pl.when(y == 0)
    def _():
        handed.wait_recv()
        slots(0, given[...])

    @pl.when(y == 1)
    def _():
        handed.wait_send()

    writes = [
        pltpu.make_async_copy(dkb, dk_ref, sem_out.at[0]),
        pltpu.make_async_copy(dvb, dv_ref, sem_out.at[1]),
        pltpu.make_async_copy(thin_d, thin_d_ref, sem_out.at[2]),
        pltpu.make_async_copy(thin_f, thin_f_ref, sem_out.at[3]),
        pltpu.make_async_copy(sums, sums_ref, sem_out.at[4]),
        *[
            pltpu.make_async_copy(tiles.at[i], first_rows(ref), sem_out.at[5 + i])
            for i, ref in enumerate(merged)
        ],
    ]
    for copy in writes:
        copy.start()
    for copy in writes + stores[-2:]:
        copy.wait()
    swap.wait()


THIN_SHAPES = (
    sds((LOCAL, 2, THIN, D), BF16),
    sds((LOCAL, 2, THIN, FF), BF16),
    sds((FIRST_MEMORY + THIN, D), F32),
)


def chain_back(place, table, attn, ffn, q, k, v, saved, g, du, df, h, send, dk, dv, da, dq, c):
    whole = sds((LOCAL, SEG, D), BF16)
    rows = pltpu.VMEM(whole.shape, BF16)
    tile = pltpu.VMEM((LOCAL, THIN, D), BF16)
    dma = lambda *shape: pltpu.SemaphoreType.DMA(shape)
    outs = pl.pallas_call(
        chain_back_kernel,
        in_specs=[SMEM, VMEM] + [ANY] * 18,
        out_specs=[ANY] * 10,
        out_shape=[whole] * 5
        + list(THIN_SHAPES)
        + [sds((2, FF, D), BF16), sds(send.shape, BF16)],
        input_output_aliases={15 + i: i for i in range(5)},
        scratch_shapes=[
            pltpu.VMEM((4, D, D), BF16),
            pltpu.VMEM((2, FF, D), BF16),
            tile,
            rows,
            rows,
            rows,
            rows,
            pltpu.VMEM((3, LOCAL, THIN, D), BF16),
            rows,
            rows,
            pltpu.VMEM((2, LOCAL, SEG, CHUNK), BF16),
            pltpu.VMEM((2, LOCAL, SEG, CHUNK), BF16),
            pltpu.VMEM((2, 2, CHUNK, D), BF16),
            *[pltpu.VMEM(s.shape, s.dtype) for s in SAVED + THIN_SHAPES],
            pltpu.VMEM((THIN, D), F32),
            pltpu.VMEM((THIN, D), F32),
            dma(3),
            dma(11),
            dma(2),
            dma(2, 2),
            dma(8),
            dma(2),
            dma(2),
            dma(2),
        ],
        name="chain_back",
        compiler_params=params(collective_id=3, has_side_effects=True),
    )(place, table, attn, ffn, q, k, v, *saved, g, du, df, h, send, dk, dv, da, dq, c)
    return outs[:5], outs[5:8], outs[8], outs[9]


def table_row(ref, index, entries):
    blocks = []
    lane = lax.broadcasted_iota(jnp.int32, (1, 128), 1)
    for block in range(D // 128):
        at, end = index * D + 128 * block, index * D + 128 * (block + 1)
        target, value = 0, jnp.zeros((1, 128), F32)
        while at < end:
            shard, inner = at // entries, at % entries
            count = min(end - at, entries - inner, 128 - inner % 128)
            place = (shard // 8, shard // 4 % 2, shard // 2 % 2, shard % 2)
            source = ref[place][inner // 128 : inner // 128 + 1]
            shift = (target - inner) % 128
            if shift:
                source = pltpu.roll(source, shift, 1)
            value = jnp.where((lane >= target) & (lane < target + count), source, value)
            at, target = at + count, target + count
        blocks.append(value)
    return jnp.concatenate(blocks, axis=1)


def head_kernel(
    nz,
    entries,
    attn_src,
    ffn_src,
    vec_src,
    tokens,
    attn_ref,
    ffn_ref,
    vec_ref,
    x_ref,
    q_ref,
    k_ref,
    v_ref,
    c_ref,
    log_ref,
    wa,
    vec,
    mine,
    other,
    xb,
    qb,
    kb,
    vb,
    cb,
    logs,
    send_sem,
    recv_sem,
    own_sem,
    swap_sem,
    out_sem,
):
    place = my_place()
    side = place[3]
    halves = swap_halves(place, tokens, other, swap_sem)
    own = [
        pltpu.make_async_copy(attn_src, attn_view(wa, *place), own_sem.at[0]),
        pltpu.make_async_copy(vec_src, vec_view(vec, *place), own_sem.at[1]),
        pltpu.make_async_copy(ffn_src, ffn_view(ffn_ref, *place), own_sem.at[2]),
        pltpu.make_async_copy(tokens.at[pl.ds(LOCAL * side, LOCAL)], mine, own_sem.at[3]),
    ]
    for copy in own:
        copy.start()
    entry_barrier(nz)
    steps = functools.partial(gather_steps, nz, place, send_sem=send_sem, recv_sem=recv_sem)
    begin, step, end_arrive, end_send = steps(
        1, True, [(0, wa, attn_view), (1, vec, vec_view)]
    )
    late = [
        steps(place[2], bool(i), [(2 + i, ffn_ref.at[i], hidden_view)]) for i in range(2)
    ]
    own[0].wait()
    own[1].wait()
    begin()
    halves.start()

    def loop(t, carry):
        step(t)
        return carry

    lax.fori_loop(1, nz + 2, loop, 0)
    own[2].wait()
    for begin2, _, _, _ in late:
        begin2()
    own[3].wait()
    halves.wait()
    end_arrive()
    outs = [
        pltpu.make_async_copy(wa, attn_ref, out_sem.at[0]),
        pltpu.make_async_copy(vec, vec_ref, out_sem.at[1]),
    ]
    for copy in outs:
        copy.start()

    weight = lambda i: wa[i].reshape(D, D)

    def project_slot(s):
        x = whole_rows(side, mine[s], other[s]).astype(BF16)
        xb[s] = x
        qb[s] = ((nn(x, weight(0)) + table_row(vec, QUERY_BIAS, entries)) * SCALE).astype(BF16)
        kb[s] = nn(x, weight(1)).astype(BF16)
        vb[s] = (nn(x, weight(2)) + table_row(vec, VALUE_BIAS, entries)).astype(BF16)
        for i, (buf, out) in enumerate(((xb, x_ref), (qb, q_ref), (kb, k_ref), (vb, v_ref))):
            outs.append(pltpu.make_async_copy(buf.at[s], out.at[s], out_sem.at[2 + 4 * s + i]))
            outs[-1].start()

    def attend_at(i, carry):
        s, h = i // (HEADS // 2), i % (HEADS // 2)
        lanes = pl.ds(pl.multiple_of(h * 2 * DH, 2 * DH), 2 * DH)
        context, log_rows = attend_pair(qb[s, :, lanes], kb[s, :, lanes], vb[s, :, lanes])
        cb[s, :, lanes] = context
        for head in range(2):
            logs[s, h, head : head + 1] = log_rows[head]
        return carry

    project_slot(0)
    project_slot(1)
    pairs = LOCAL * HEADS // 2
    done = 0
    for t in range(1, nz + 2):
        for _, step2, _, _ in late:
            step2(t)
        upto = pairs * t // (nz + 1)
        lax.fori_loop(done, upto, attend_at, 0)
        done = upto
    outs.append(pltpu.make_async_copy(cb, c_ref, out_sem.at[2 + 4 * LOCAL]))
    outs.append(pltpu.make_async_copy(logs, log_ref, out_sem.at[3 + 4 * LOCAL]))
    outs[-1].start()
    outs[-2].start()
    end_send()
    for _, _, end_arrive2, end_send2 in late:
        end_send2()
        end_arrive2()
    for copy in outs:
        copy.wait()


def head(nz, attention, hidden_major, vec, tokens, entries):
    rows, hidden = attention.shape[1], hidden_major.shape[1]
    whole = sds((LOCAL, SEG, D), BF16)
    logs = (LOCAL, HEADS // 2, 2, SEG)
    attn_shape, vec_shape = (4, nz, 2, 2, rows, D), (nz, 2, 2, 2, *VEC_TILE)
    half = pltpu.VMEM((LOCAL, *tokens.shape[1:]), BF16)
    return pl.pallas_call(
        functools.partial(head_kernel, nz, entries),
        in_specs=[ANY] * 4,
        out_specs=[ANY] * 9,
        out_shape=[
            sds(attn_shape, BF16),
            sds((2, nz, 2, 2, 2, hidden, D), BF16),
            sds(vec_shape, F32),
            *[whole] * 5,
            sds(logs, F32),
        ],
        scratch_shapes=[
            pltpu.VMEM(attn_shape, BF16),
            pltpu.VMEM(vec_shape, F32),
            half,
            half,
            *[pltpu.VMEM(whole.shape, BF16)] * 5,
            pltpu.VMEM(logs, F32),
            pltpu.SemaphoreType.DMA((11, nz, 4)),
            pltpu.SemaphoreType.DMA((8, nz, 4)),
            pltpu.SemaphoreType.DMA((4,)),
            pltpu.SemaphoreType.DMA((2,)),
            pltpu.SemaphoreType.DMA((4 + 4 * LOCAL,)),
        ],
        name="head",
        compiler_params=params(collective_id=0, has_side_effects=True),
    )(attention, hidden_major, vec, tokens)


def token_grad_kernel(place_ref, da_ref, dq_ref, dk_ref, dv_ref, w_ref, keep_ref, send_ref):
    side = lax.axis_index("tensor")
    total = da_ref[0].astype(F32)
    for i, ref in enumerate((dq_ref, dk_ref, dv_ref)):
        total = total + nt(ref[0], w_ref[i])
    live = place_ref[LOCAL * side + pl.program_id(0)] >= 0
    keep, send = split_rows(side, jnp.where(live, total, 0.0))
    keep_ref[0] = keep.astype(BF16)
    send_ref[0] = send.astype(BF16)


def token_gradient(place, da, dq, dk, dv, attn):
    half = (SEG - MEM) // 2
    return pl.pallas_call(
        token_grad_kernel,
        grid=(LOCAL,),
        in_specs=[SMEM] + [slot_rows()] * 4 + [once((3, D, D), (0, 0, 0))],
        out_specs=[half_rows(half)] * 2,
        out_shape=[sds((LOCAL, half, D), BF16)] * 2,
        name="token_gradient",
        compiler_params=params(),
    )(place, da, dq, dk, dv, attn)


def flat(ref):
    return ref[...].reshape(LOCAL * ref.shape[1], ref.shape[2])


def attn_grad_kernel(
    x_ref, da_ref, dq_ref, dk_ref, dv_ref, c_ref, sums_ref, thin_sums_ref, out_ref, vec_ref
):
    x = flat(x_ref)
    dq, dv = flat(dq_ref), flat(dv_ref)
    out_ref[0] = tn(x, dq).astype(BF16)
    out_ref[1] = tn(x, flat(dk_ref)).astype(BF16)
    out_ref[2] = tn(x, dv).astype(BF16)
    out_ref[3] = tn(flat(da_ref), flat(c_ref)).astype(BF16)
    vec_ref[...] = thin_sums_ref[...]
    vec_ref[0:FIRST_MEMORY] = thin_sums_ref[0:FIRST_MEMORY] + sums_ref[0:FIRST_MEMORY]
    vec_ref[QUERY_BIAS : QUERY_BIAS + 1] = row_sum(dq.astype(F32))
    vec_ref[VALUE_BIAS : VALUE_BIAS + 1] = row_sum(dv.astype(F32))


def attn_gradient(x, da, dq, dk, dv, c, sums, thin_sums, chunk=256):
    part = pl.BlockSpec((LOCAL, SEG, chunk), lambda i: (0, 0, i))
    full = once((LOCAL, SEG, D), (0, 0, 0))
    lanes = lambda rows: pl.BlockSpec((rows, chunk), lambda i: (0, i))
    return pl.pallas_call(
        attn_grad_kernel,
        grid=(D // chunk,),
        in_specs=[full, full, part, part, part, part, lanes(THIN), lanes(FIRST_MEMORY + THIN)],
        out_specs=[
            pl.BlockSpec((4, D, chunk), lambda i: (0, 0, i)),
            lanes(FIRST_MEMORY + THIN),
        ],
        out_shape=[sds((4, D, D), BF16), sds((FIRST_MEMORY + THIN, D), F32)],
        name="attn_gradient",
        compiler_params=params(),
    )(x, da, dq, dk, dv, c, sums, thin_sums)


def add_thin_kernel(thin_f_ref, thin_d_ref, terms_ref, out_ref):
    out_ref[...] = terms_ref[...]

    @pl.when(lax.axis_index("tensor") == 0)
    def _():
        for j, (a, b) in enumerate(((0, 1), (1, 0))):
            left = jnp.concatenate([thin_f_ref[s, a] for s in range(LOCAL)], axis=0)
            right = jnp.concatenate([thin_d_ref[s, b] for s in range(LOCAL)], axis=0)
            out_ref[j] = (terms_ref[j].astype(F32) + tn(left, right)).astype(BF16)


def add_thin(terms, thin_d, thin_f):
    block = pl.BlockSpec((2, CHUNK, D), lambda i: (0, i, 0))
    return pl.pallas_call(
        add_thin_kernel,
        grid=(FF // CHUNK,),
        in_specs=[
            pl.BlockSpec((LOCAL, 2, THIN, CHUNK), lambda i: (0, 0, 0, i)),
            once(thin_d.shape, (0, 0, 0, 0)),
            block,
        ],
        out_specs=block,
        out_shape=sds((2, FF, D), BF16),
        name="add_thin",
        compiler_params=params(),
    )(thin_f, thin_d, terms)


def update(gradient, momentum, weight, average, rate, grad_scale):
    scaled = gradient * grad_scale
    moment = MOMENTUM * momentum + scaled
    weight_new = weight - rate * (scaled + MOMENTUM * moment)
    return (moment, weight_new, AVERAGE_DECAY * average + (1.0 - AVERAGE_DECAY) * weight_new)


VEC_TILE = (8, 128)


def in_tiles(rows):
    size = VEC_TILE[0] * VEC_TILE[1]
    padded = jnp.pad(rows, [(0, 0)] * (rows.ndim - 1) + [(0, size - rows.shape[-1])])
    return padded.reshape(*rows.shape[:-1], *VEC_TILE)


def start(attention, feedforward, vectors, tokens):
    nz = lax.axis_size("dp") // 4
    rows, hidden, entries = attention.shape[1], feedforward.shape[2], vectors.shape[0]
    attention = attention.astype(BF16)
    hidden_major = jnp.swapaxes(feedforward.astype(BF16), 1, 2)
    vec = in_tiles(vectors.astype(BF16).astype(F32))
    aligned = rows % THIN == 0
    if aligned:
        attn, ffn, table, *work = head(nz, attention, hidden_major, vec, tokens, entries)
    else:
        attn, ffn, table, other = gather(
            nz,
            0,
            [
                (attention, (4, nz, 2, 2, rows, D), attn_view),
                (hidden_major, (2, nz, 2, 2, 2, hidden, D), ffn_view),
                (vec, (nz, 2, 2, 2, *VEC_TILE), vec_view),
            ],
            tokens,
        )
    attn, ffn = attn.reshape(4, D, D), ffn.reshape(2, FF, D)
    table = table.reshape(nz * 8, VEC_TILE[0] * VEC_TILE[1])[:, :entries].reshape(NVEC, D)
    if not aligned:
        work = project(tokens, other, attn, table)
        work = [*work, *attend(*work[1:])]
    return attn, ffn, table, work


def scatter_gradients(attn_terms, ffn_terms, vec_terms, shapes):
    nz = lax.axis_size("dp") // 4
    rows, hidden, entries = shapes
    attn, ffn, vec = scatter(
        nz,
        1,
        [
            (attn_terms.reshape(4, nz, 2, 2, rows, D), (4, rows, HALF), attn_view),
            (ffn_terms.reshape(2, nz, 2, 2, 2, hidden, D), (2, hidden, D), ffn_view),
            (in_tiles(vec_terms.reshape(nz, 2, 2, 2, entries)), VEC_TILE, vec_view),
        ],
    )
    return attn.astype(F32), jnp.swapaxes(ffn, 1, 2).astype(F32), vec.reshape(-1)[:entries]


def swap(value):
    return lax.ppermute(value, "tensor", [(0, 1), (1, 0)])


def joined_kernel(keep_ref, other_ref, out_ref, sem):
    side = lax.axis_index("tensor")
    copies = [
        pltpu.make_async_copy(keep_ref, out_ref.at[pl.ds(LOCAL * side, LOCAL)], sem.at[0]),
        pltpu.make_async_copy(other_ref, out_ref.at[pl.ds(LOCAL * (1 - side), LOCAL)], sem.at[1]),
    ]
    for c in copies:
        c.start()
    for c in copies:
        c.wait()


def joined(keep, other):
    return pl.pallas_call(
        joined_kernel,
        in_specs=[ANY] * 2,
        out_specs=ANY,
        out_shape=sds((2 * LOCAL, *keep.shape[1:]), keep.dtype),
        scratch_shapes=[pltpu.SemaphoreType.DMA((2,))],
        name="joined",
        compiler_params=params(16),
    )(keep, other)


def on_device(
    tokens,
    slot_position,
    cotangent,
    attention,
    feedforward,
    vectors,
    attn_momentum,
    ffn_momentum,
    vec_momentum,
    attn_average,
    ffn_average,
    vec_average,
):
    place = slot_position
    attn, ffn, table, work = start(attention, feedforward, vectors, tokens)
    x, q, k, v, c, log_tokens = work

    (x, q, k, v), saved, cot_other = chain(place, table, attn, ffn, x, q, k, v, cotangent)
    keep, send, h, g, du, df, da, dc, c, log_total, sums = rows_part(
        place, x, q, k, v, c, log_tokens, cotangent, cot_other, attn, ffn, table
    )
    dq, dk, dv = attend_back(q, k, v, dc, log_total)
    (dk, dv, da, dq, c), thin, ffn_terms, received = chain_back(
        place, table, attn, ffn, q, k, v, saved, g, du, df, h, send, dk, dv, da, dq, c
    )
    thin_d, thin_f, thin_sums = thin
    activations = joined(keep, received)

    keep, send = token_gradient(place, da, dq, dk, dv, attn)
    token_grad = joined(keep, swap(send))
    ffn_terms = add_thin(ffn_terms, thin_d, thin_f)
    attn_terms, vec_terms = attn_gradient(x, da, dq, dk, dv, c, sums, thin_sums)
    vec_terms = vec_terms[:NVEC]

    attn_grad, ffn_grad, vec_grad = scatter_gradients(
        attn_terms,
        ffn_terms,
        vec_terms,
        (attention.shape[1], feedforward.shape[2], vectors.shape[0]),
    )
    grad_scale = 1.0 / math.sqrt(lax.axis_size("dp") * SLOTS * ROWS)
    attn_new = update(attn_grad, attn_momentum, attention, attn_average, ATTENTION_RATE, grad_scale)
    ffn_new = update(ffn_grad, ffn_momentum, feedforward, ffn_average, FEEDFORWARD_RATE, grad_scale)
    vec_new = update(vec_grad, vec_momentum, vectors, vec_average, VECTOR_RATE, grad_scale)
    return (
        activations,
        token_grad,
        attn_new[0],
        ffn_new[0],
        vec_new[0],
        attn_new[1],
        ffn_new[1],
        vec_new[1],
        attn_new[2],
        ffn_new[2],
        vec_new[2],
    )


def solution(mesh):
    attn_spec = P(None, "dp", "tensor")
    ffn_spec = P(None, None, ("dp", "tensor"))
    vec_spec = P(("dp", "tensor"))
    rows_spec = P("dp", "tensor", None)
    states = (attn_spec, ffn_spec, vec_spec)
    return jax.shard_map(
        on_device,
        mesh=mesh,
        in_specs=(rows_spec, P("dp"), rows_spec) + states * 3,
        out_specs=(rows_spec, rows_spec) + states * 3,
        check_vma=False,
    )
```

profile of v0, /device:TPU:1, one launch (start us, length us, event | category | flops | bytes accessed | tf_op | source)
XLA Modules:
  0.0 349.1 jit_solution(7352515694649699484)
XLA Ops:
  1.9 1.6 convert_element_type.21.attn_src
  3.6 1.8 convert_bitcast_fusion.ffn_src
  5.4 2.9 copy.38.cot_ref.mine_ref
  8.2 1.4 copy.37.tokens
  9.6 74.7 %head.1 = (bf16[4,4,2,2,48,768]{5,4,3,2,1,0:T(8,128)(2,1)}, bf16[2,4,2,2,2,96,768]{6,5,4,3,2,1,0:T(8,128)(2,1)}, f32[4,2,2,2,8,128]{5,4,3,2,1,0:T(8,128)}, bf16[...) custom-call(bf16[4,48,384]{2,1,0:T(8,128)(2,1)} %convert_element_typ, ...), custom_call_target="tpu_custom_call" | custom-call | tf_op jit(solution)/shard_map/head/pallas_call | solution.py:1609
  84.3 0.9 copy.46
  86.0 19.6 %chain.1 = (bf16[2,512,768]{2,1,0:T(8,128)(2,1)}, bf16[2,512,768]{2,1,0:T(8,128)(2,1)}, bf16[2,512,768]{2,1,0:T(8,128)(2,1)}, bf16[2,512,768]{2,1,0:T(8,128)(2,1...) custom-call(s32[4]{0:T(128)} %place_ref.7, ...), custom_call_target="tpu_custom_call", output_to_operand_aliasing={{0}: (4, {}), {1}: (5, {}), {2}: (6, {}), {3}: (7, {})} | custom-call | tf_op jit(solution)/shard_map/chain/pallas_call | solution.py:886
  105.6 58.0 %rows_part.1 = (bf16[2,251,768]{2,1,0:T(8,128)(2,1)}, bf16[2,251,768]{2,1,0:T(8,128)(2,1)}, bf16[2,512,768]{2,1,0:T(8,128)(2,1)}, bf16[2,512,3072]{2,1,0:T(8,128...) custom-call(s32[4]{0:T(128)} %place_ref.7, ...), custom_call_target="tpu_custom_call" | custom-call | tf_op jit(solution)/shard_map/rows_part/pallas_call | solution.py:1134
  163.6 24.1 %attend_back.1 = (bf16[2,512,768]{2,1,0:T(8,128)(2,1)}, bf16[2,512,768]{2,1,0:T(8,128)(2,1)}, bf16[2,512,768]{2,1,0:T(8,128)(2,1)}) custom-call(bf16[2,512,768]{2,1,0:T(8,128)(2,1)} %get-tuple-element.67.q_ref, bf16[2,512,768]{2,1,0:T(8,128)(2,1)} %get-tuple-element.68.k16_ref.k_ref, bf16[2,512,768]{2,1,0:T(8,128)(2,1)} %get-tuple-element.69.v16_ref.v_ref, ...), custom_call_target="tpu_custom_call" | custom-call | tf_op jit(solution)/shard_map/attend_back/pallas_call | solution.py:1030
  187.7 40.2 %chain_back.1 = (bf16[2,512,768]{2,1,0:T(8,128)(2,1)}, bf16[2,512,768]{2,1,0:T(8,128)(2,1)}, bf16[2,512,768]{2,1,0:T(8,128)(2,1)}, bf16[2,512,768]{2,1,0:T(8,128...) custom-call(s32[4]{0:T(128)} %place_ref.7, ...), custom_call_target="tpu_custom_call", output_to_operand_aliasing={{0}: (15, {}), {1}: (16, {}), {2}: (17, {}), {3}: (18, {}),... | custom-call | tf_op jit(solution)/shard_map/chain_back/pallas_call | solution.py:1426
  227.9 9.0 %token_gradient.1 = (bf16[2,251,768]{2,1,0:T(8,128)(2,1)}, bf16[2,251,768]{2,1,0:T(8,128)(2,1)}) custom-call(s32[4]{0:T(128)} %place_ref.7, bf16[2,512,768]{2,1,0:T(8,128)(2,1)} %get-tuple-element.90.da_ref, bf16[2,512,768]{2,1,0:T(8,128)(2,1)} %get-tuple-element.91.dq_ref, bf16[2,512,768]{2,1,0:T(8,128)(2,1)} %get-tuple-element.92.dk_ref, ...), custom_call_target="tpu_custom_call" | custom-call | tf_op jit(solution)/shard_map/token_gradient/pallas_call | solution.py:1651
  236.9 2.0 copy.40
  238.9 2.6 collective-permute-start
  241.6 2.3 copy.42
  243.9 10.1 %attn_gradient.1 = (bf16[4,768,768]{2,1,0:T(8,128)(2,1)}, f32[28,768]{1,0:T(8,128)}) custom-call(bf16[2,512,768]{2,1,0:T(8,128)(2,1)} %get-tuple-element.66.x_ref, bf16[2,512,768]{2,1,0:T(8,128)(2,1)} %get-tuple-element.90.da_ref, bf16[2,512,768]{2,1,0:T(8,128)(2,1)} %get-tuple-element.91.dq_ref, bf16[2,512,768]{2,1,0:T(8,128)(2,1)} %get-tuple-element.92.dk_ref, ...), custom_call_target="tpu_custom_call" | custom-call | tf_op jit(solution)/shard_map/attn_gradient/pallas_call | solution.py:1685
  254.0 0.9 slice.10
  255.1 0.8 reshape.63.refs_2_
  255.9 9.5 %add_thin.1 = bf16[2,3072,768]{2,1,0:T(8,128)(2,1)} custom-call(bf16[2,2,16,3072]{3,2,1,0:T(8,128)(2,1)} %get-tuple-element.100.thin_f_ref, bf16[2,2,16,768]{3,2,1,0:T(8,128)(2,1)} %get-tuple-element.101.thin_d_ref, bf16[2,3072,768]{2,1,0:T(8,128)(2,1)} %get-tuple-element.102.terms_ref), custom_call_target="tpu_custom_call" | custom-call | tf_op jit(solution)/shard_map/add_thin/pallas_call | solution.py:1712
  265.4 73.8 %scatter.1 = (bf16[4,48,384]{2,1,0:T(8,128)(2,1)}, bf16[2,96,768]{2,1,0:T(8,128)(2,1)}, f32[8,128]{1,0:T(8,128)}) custom-call(bf16[4,4,2,2,48,768]{5,4,3,2,1,0:T(8,128)(2,1)} %bitcast.32, bf16[2,4,2,2,2,96,768]{6,5,4,3,2,1,0:T(8,128)(2,1)} %bitcast.31, f32[4,2,2,2,8,128]{5,4,3,2,1,0:T(8,128)} %reshape.63.refs_2_), custom_call_target="tpu_custom_call" | custom-call | tf_op jit(solution)/shard_map/scatter/pallas_call | solution.py:612
  339.3 1.4 multiply_add_fusion.2
  340.7 2.1 multiply_add_fusion.1
  342.9 2.4 multiply_add_fusion
  345.3 1.0 copy-done
  346.5 2.3 copy.43
  (31 shorter events, 2.6 us)
Async XLA Ops:
  5.4 2.9 copy-start.4
  227.9 13.6 %copy-start.2 = (bf16[2,251,768]{2,1,0:T(8,128)(2,1)S(1)}, bf16[2,251,768]{2,1,0:T(8,128)(2,1)}, u32[]{:S(2)}) copy-start(bf16[2,251,768]{2,1,0:T(8,128)(2,1)} %get-tuple-element.89.other_ref) | copy-start | bytes 2313220
  236.9 4.6 %copy-start.1 = (bf16[2,251,768]{2,1,0:T(8,128)(2,1)S(1)}, bf16[2,251,768]{2,1,0:T(8,128)(2,1)}, u32[]{:S(2)}) copy-start(bf16[2,251,768]{2,1,0:T(8,128)(2,1)} %get-tuple-element.73.keep_ref) | copy-start | bytes 2313220
  238.9 106.4 %collective-permute-start = (bf16[2,251,768]{2,0,1:T(2,128)(2,1)S(1)}, bf16[2,251,768]{2,0,1:T(2,128)(2,1)S(1)}, u32[]{:S(2)}, u32[]{:S(2)}) collective-permute-start(bf16[2,251,768]{2,0,1:T(2,128)(2,1)S(1)} %copy.40), channel_id=1, source_target_pairs={{0,1},{1,0},{2,3},{3,2},{4,5},{5,4},{6,7},{7,6},{8,9},{9,8},{10,11... | collective-permute-start | bytes 2313224 | tf_op jit(solution)/shard_map/ppermute | solution.py:1787
  265.4 73.9 %copy-start.8 = (f32[528]{0:T(1024)S(1)}, f32[528]{0:T(1024)}, u32[]{:S(2)}) copy-start(f32[528]{0:T(1024)} %param.17) | copy-start | bytes 6340
  265.4 73.9 %copy-start.9 = (f32[528]{0:T(1024)S(1)}, f32[528]{0:T(1024)}, u32[]{:S(2)}) copy-start(f32[528]{0:T(1024)} %param.23) | copy-start | bytes 6340
  265.4 73.9 %copy-start.10 = (f32[528]{0:T(1024)S(1)}, f32[528]{0:T(1024)}, u32[]{:S(2)}) copy-start(f32[528]{0:T(1024)} %param.20) | copy-start | bytes 6340
  265.4 75.3 %copy-start.5 = (f32[4,48,384]{2,1,0:T(8,128)S(1)}, f32[4,48,384]{2,1,0:T(8,128)}, u32[]{:S(2)}) copy-start(f32[4,48,384]{2,1,0:T(8,128)} %param.15) | copy-start | bytes 884740
  339.3 3.6 %copy-start.3 = (f32[2,768,96]{1,2,0:T(8,128)S(1)}, f32[2,768,96]{1,2,0:T(8,128)}, u32[]{:S(2)}) copy-start(f32[2,768,96]{1,2,0:T(8,128)} %param.16) | copy-start | bytes 1769476
  339.3 3.6 %copy-start.6 = (f32[2,768,96]{1,2,0:T(8,128)S(1)}, f32[2,768,96]{1,2,0:T(8,128)}, u32[]{:S(2)}) copy-start(f32[2,768,96]{1,2,0:T(8,128)} %param.22) | copy-start | bytes 1769476
  339.3 3.6 %copy-start.7 = (f32[2,768,96]{1,2,0:T(8,128)S(1)}, f32[2,768,96]{1,2,0:T(8,128)}, u32[]{:S(2)}) copy-start(f32[2,768,96]{1,2,0:T(8,128)} %param.19) | copy-start | bytes 1769476
  345.2 1.1 copy-start
where the time goes:
time: 352 us; the launch traced here: 349 us
  Pallas kernels  319 us (91%)
  local copies, waits for them, and re-layouts  15.6 us (4%)
  other arithmetic  10.6 us (3%)
    pallas_call x1, Pallas kernels, head(): pl.pallas_call(functools.partial(head_kernel, nz, entries), in_specs=[ANY...  74.7 us
    pallas_call x1, Pallas kernels, scatter(): pl.pallas_call(functools.partial(scatter_kernel, nz, views), in_specs=[AN...  73.8 us
    pallas_call x1, Pallas kernels, rows_part(): pl.pallas_call(rows_kernel, grid=(LOCAL,), in_specs=[SMEM, rows, rows, th...  58 us
    pallas_call x1, Pallas kernels, chain_back(): pl.pallas_call(chain_back_kernel, in_specs=[SMEM, VMEM] + [ANY] * 18, out...  40.2 us
    pallas_call x1, Pallas kernels, attend_back(): pl.pallas_call(attend_back_kernel, grid=(LOCAL, HEADS // 2), in_specs=[PA...  24.1 us
    pallas_call x1, Pallas kernels, chain(): pl.pallas_call(chain_kernel, in_specs=[SMEM, VMEM] + [ANY] * 7, out_specs...  19.6 us
    unnamed x27, local copies, waits for them, and re-layouts  10.9 us
    pallas_call x1, Pallas kernels, attn_gradient(): pl.pallas_call(attn_grad_kernel, grid=(D // chunk,), in_specs=[full, full...  10.1 us
  transfers between devices with their start and end apart: 1, of which 0 were waited for; matrix products, arithmetic and copies ran while one was open for 3% of the time, Pallas kernels for 27%

commit v1 on v0

--- a/solution.py
+++ b/solution.py
@@ -353,6 +353,15 @@
         sem.at[1],
         device(z, x, c, 1 - y),
     )
+
+
+def place_rows(place, keep, send, out, sem):
+    z, x, c, y = place
+    own = out.at[pl.ds(LOCAL * y, LOCAL)]
+    return [
+        pltpu.make_async_copy(keep, own, sem.at[2]),
+        remote(send, own, sem.at[0], sem.at[1], device(z, x, c, 1 - y)),
+    ]
 
 
 def gather_kernel(nz, views, *refs):
@@ -989,53 +998,39 @@
     )(q, k, v)
 
 
-def attend_back_kernel(q_ref, k_ref, v_ref, dc_ref, log_ref, dq_ref, dk_ref, dv_ref):
+def attend_back_pair(q, k, v, dc, logs):
     last = SEG // TILE
-    key_terms, value_terms = [], []
+    key_terms, value_terms, query_terms = [], [], []
     for head in range(2):
-        key_sum, value_sum = [], []
-        query_parts = []
+        key_sum, value_sum, query_parts = [], [], []
         for part in range(last):
             rows = slice(TILE * part, TILE * (part + 1))
             keys = slice(0, TILE * (part + 1))
-            q, dc = q_ref[0, rows], dc_ref[0, rows]
-            k = k_ref[0, keys]
-            score = nt(own_lanes(k, head), q)
-            share = jnp.exp(score - log_ref[0, 0, head : head + 1, rows])
+            score = nt(own_lanes(k[keys], head), q[rows])
+            share = jnp.exp(score - logs[head : head + 1, rows])
             share = jnp.where(seen(score, TILE * part), share, 0.0)
-            share_grad = nt(own_lanes(v_ref[0, keys], head), dc)
+            share_grad = nt(own_lanes(v[keys], head), dc[rows])
             inner = jnp.sum(share_grad * share, axis=0, keepdims=True)
             score_grad = (share * (share_grad - inner)).astype(BF16)
-            value_sum.append(nn(share.astype(BF16), dc))
-            key_sum.append(nn(score_grad, q))
-            query_parts.append(tn(score_grad, k))
+            value_sum.append(nn(share.astype(BF16), dc[rows]))
+            key_sum.append(nn(score_grad, q[rows]))
+            query_parts.append(tn(score_grad, k[keys]))
         key_terms.append(key_sum)
         value_terms.append(value_sum)
-        if head == 0:
-            first_queries = query_parts
+        query_terms.append(query_parts)
+    lane = lax.broadcasted_iota(jnp.int32, (TILE, 2 * DH), 1)
+    pick = lambda a, b: jnp.where(lane < DH, a, b)
+    dq, dk, dv = [], [], []
     for part in range(last):
         rows = slice(TILE * part, TILE * (part + 1))
-        lane = lax.broadcasted_iota(jnp.int32, (TILE, 2 * DH), 1)
-        pick = lambda a, b: jnp.where(lane < DH, a, b)
-        dq_ref[0, rows] = (pick(first_queries[part], query_parts[part]) * SCALE).astype(BF16)
-        for terms, out in ((key_terms, dk_ref), (value_terms, dv_ref)):
+        dq.append((pick(query_terms[0][part], query_terms[1][part]) * SCALE).astype(BF16))
+        for terms, out in ((key_terms, dk), (value_terms, dv)):
             total = None
             for later in range(part, last):
                 term = pick(terms[0][later][rows], terms[1][later][rows])
                 total = term if total is None else total + term
-            out[0, rows] = total.astype(BF16)
-
-
-def attend_back(q, k, v, dc, log_total):
-    return pl.pallas_call(
-        attend_back_kernel,
-        grid=(LOCAL, HEADS // 2),
-        in_specs=[PAIR] * 4 + [PAIR_LOG],
-        out_specs=[PAIR] * 3,
-        out_shape=[sds((LOCAL, SEG, D), BF16)] * 3,
-        name="attend_back",
-        compiler_params=params(),
-    )(q, k, v, dc, log_total)
+            out.append(total)
+    return [jnp.concatenate(parts, axis=0) for parts in (dq, dk, dv)]
 
 
 def rows_kernel(
@@ -1150,6 +1145,24 @@
 CHUNK = 768
 
 
+def memory_key_gradient(q, k16, v16, dc, context, logs, masks):
+    score = nt(by_head(k16, masks), q).reshape(HEADS, THIN, SEG)
+    key = lax.broadcasted_iota(jnp.int32, score.shape, 1)
+    share = jnp.where(key < MEM, jnp.exp(score - logs[:, None]), 0.0)
+    share_grad = nt(by_head(v16, masks), dc).reshape(HEADS, THIN, SEG)
+    product = dc.astype(F32) * context.astype(F32)
+    coarse = product.astype(BF16)
+    fine = (product - coarse.astype(F32)).astype(BF16)
+    head = lax.broadcasted_iota(jnp.int32, (THIN, D), 0)
+    ones = jnp.where(head == lax.broadcasted_iota(jnp.int32, (THIN, D), 1) // DH, 1.0, 0.0)
+    ones = ones.astype(BF16)
+    inner = (nt(ones, coarse) + nt(ones, fine))[0:HEADS]
+    score_grad = (share * (share_grad - inner[:, None])).reshape(HEADS * THIN, SEG)
+    share = share.reshape(HEADS * THIN, SEG).astype(BF16)
+    dk = own_columns(nn(score_grad.astype(BF16), q), masks)
+    return dk, own_columns(nn(share, dc), masks)
+
+
 def chain_back_kernel(
     place_ref,
     table_ref,
@@ -1165,27 +1178,29 @@
     du_ref,
     df_ref,
     h_ref,
+    keep_ref,
     send_ref,
-    dk_in,
-    dv_in,
+    dc_ref,
+    log_ref,
     da_in,
-    dq_in,
     c_in,
+    da_ref,
+    c_ref,
+    dq_ref,
     dk_ref,
     dv_ref,
-    da_ref,
-    dq_ref,
-    c_ref,
-    thin_d_ref,
-    thin_f_ref,
     sums_ref,
     terms_ref,
-    received_ref,
+    rows_ref,
     wa,
     wf,
     qb,
     kb,
     vb,
+    dcb,
+    cb,
+    logs,
+    dqb,
     dkb,
     dvb,
     tiles,
@@ -1211,7 +1226,7 @@
     sem_grad,
     sem_swap,
 ):
-    del dk_in, dv_in, da_in, dq_in, c_in
+    del da_in, c_in
     place = z, x, c, y = my_place()
     loads = [
         pltpu.make_async_copy(attn_ref, wa, sem_w.at[0]),
@@ -1219,23 +1234,20 @@
         pltpu.make_async_copy(ffn_ref.at[1], wf.at[1], sem_w.at[2]),
     ]
     first_rows = lambda ref: ref.at[:, pl.ds(0, THIN)]
-    grads = [
-        pltpu.make_async_copy(dk_ref, dkb, sem_in.at[0]),
-        pltpu.make_async_copy(dv_ref, dvb, sem_in.at[1]),
-    ]
     saved = [
         pltpu.make_async_copy(saved_d_ref, save_d, sem_in.at[2]),
         pltpu.make_async_copy(saved_f_ref, save_f, sem_in.at[3]),
         pltpu.make_async_copy(saved_s_ref, save_s, sem_in.at[4]),
     ]
     reads = [
-        pltpu.make_async_copy(first_rows(q_ref), qb, sem_in.at[5]),
-        pltpu.make_async_copy(k_ref, kb, sem_in.at[6]),
-        pltpu.make_async_copy(v_ref, vb, sem_in.at[7]),
+        pltpu.make_async_copy(src, dst, sem_in.at[5 + i])
+        for i, (src, dst) in enumerate(
+            ((q_ref, qb), (k_ref, kb), (v_ref, vb), (dc_ref, dcb), (c_ref, cb), (log_ref, logs))
+        )
     ]
-    merged = (da_ref, dq_ref, c_ref)
+    merged = (da_ref, c_ref)
     tile_reads = [
-        pltpu.make_async_copy(first_rows(ref), tiles.at[i], sem_in.at[8 + i])
+        pltpu.make_async_copy(first_rows(ref), tiles.at[i], sem_in.at[i])
         for i, ref in enumerate(merged)
     ]
     rows_in = [
@@ -1244,15 +1256,16 @@
     ]
 
     def chunk_reads(i):
-        lanes = pl.ds(CHUNK * i, CHUNK)
+        lanes = pl.ds(pl.multiple_of(CHUNK * i, CHUNK), CHUNK)
+        slot = lax.rem(i, 2)
         return [
-            pltpu.make_async_copy(src.at[:, :, lanes], dst.at[i % 2], sem_chunk.at[i % 2, j])
+            pltpu.make_async_copy(src.at[:, :, lanes], dst.at[slot], sem_chunk.at[slot, j])
             for j, (src, dst) in enumerate(((g_ref, gb), (du_ref, dub)))
         ]
 
     @pl.when(y == 1)
     def _():
-        for copy in grads + loads[:1] + saved + loads[:0:-1] + reads + tile_reads:
+        for copy in reads + loads[:1] + saved + loads[:0:-1] + tile_reads:
             copy.start()
         for copy in rows_in + chunk_reads(0) + chunk_reads(1):
             copy.start()
@@ -1261,25 +1274,45 @@
     def _():
         for copy in rows_in + chunk_reads(0) + chunk_reads(1):
             copy.start()
-        for copy in grads + loads[:1] + saved + loads[:0:-1] + reads + tile_reads:
+        for copy in reads + saved + loads[:0:-1] + loads[:1] + tile_reads:
             copy.start()
 
     pair_barrier(place)
-    swap = remote(
-        send_ref, received_ref, sem_swap.at[0], sem_swap.at[1], device(z, x, c, 1 - y)
-    )
-    swap.start()
+    swap = place_rows(place, keep_ref, send_ref, rows_ref, sem_swap)
+    for copy in swap:
+        copy.start()
     handed = remote(left, given, sem_grad.at[0], sem_grad.at[1], device(z, x, c, 1 - y))
 
     sums[...] = jnp.zeros_like(sums)
     thin_d[...] = jnp.zeros_like(thin_d)
     thin_f[...] = jnp.zeros_like(thin_f)
+    for buf in (dqb, dkb, dvb):
+        buf[...] = jnp.zeros_like(buf)
     masks = head_masks()
     memory_row = lax.broadcasted_iota(jnp.int32, (THIN, 1), 0) < MEM
     row = lambda r: table_ref[r : r + 1, :]
 
     def add(r, value):
         sums[r : r + 1, :] += value
+
+    def attend_at(i, carry):
+        s, h = i // (HEADS // 2), lax.rem(i, HEADS // 2)
+        lanes = pl.ds(pl.multiple_of(h * 2 * DH, 2 * DH), 2 * DH)
+        pair = (buf[s, :, lanes] for buf in (qb, kb, vb, dcb))
+        dq, dk, dv = attend_back_pair(*pair, logs[s, h])
+        dqb[s, THIN:, lanes] = dq[THIN:]
+        dqb[s, 0:THIN, lanes] = jnp.where(memory_row, dqb[s, 0:THIN, lanes], dq[0:THIN])
+        dkb[s, :, lanes] = (dk + dkb[s, :, lanes].astype(F32)).astype(BF16)
+        dvb[s, :, lanes] = (dv + dvb[s, :, lanes].astype(F32)).astype(BF16)
+        return carry
+
+    pairs = LOCAL * HEADS // 2
+
+    def key_gradient(s):
+        rows = jnp.concatenate([logs[s, h] for h in range(HEADS // 2)], axis=0)
+        return memory_key_gradient(
+            qb[s], kb[s, 0:THIN], vb[s, 0:THIN], dcb[s], cb[s], rows, masks
+        )
 
     def slots(turn, grad):
         waited = set()
@@ -1322,83 +1355,56 @@
                 need(loads[0])
                 context_grad = nn(branch_grad, wa[3]).astype(BF16)
                 dc_heads = by_head(context_grad, masks)
-                need(*reads)
-                q_heads = by_head(qb[s], masks)
+                q_heads = by_head(qb[s, 0:THIN], masks)
                 score = nt(q_heads, kb[s])
                 share = jnp.exp(score - log_total) * copies_of(score.shape)
                 share_grad = nt(dc_heads, vb[s])
                 inner = jnp.sum(share_grad * share, axis=-1, keepdims=True)
                 score_grad = (share * (share_grad - inner)).astype(BF16)
                 query_grad = (own_columns(nn(score_grad, kb[s]), masks) * SCALE).astype(BF16)
-                need(*grads)
                 dkb[s] = (dkb[s].astype(F32) + tn(score_grad, q_heads)).astype(BF16)
                 dvb[s] = (dvb[s].astype(F32) + tn(share.astype(BF16), dc_heads)).astype(BF16)
+                dqb[s, 0:THIN] = jnp.where(memory_row, query_grad, dqb[s, 0:THIN])
                 thin_d[s, 0] = down_grad
                 thin_d[s, 1] = save_d[s, 0]
                 thin_f[s, 0] = up_grad
                 thin_f[s, 1] = save_f[s, 0]
                 need(*tile_reads)
-                for i, value in enumerate((branch_grad, query_grad, save_d[s, 3])):
+                for i, value in enumerate((branch_grad, save_d[s, 3])):
                     tiles[i, s] = jnp.where(memory_row, value, tiles[i, s])
                 grad = pre_grad + nt(query_grad, wa[0])
-            need(loads[0], *grads)
-            grad = grad + nt(dkb[s, 0:THIN], wa[1]) + nt(dvb[s, 0:THIN], wa[2])
+            need(loads[0])
+            dk, dv = dkb[s, 0:THIN], dvb[s, 0:THIN]
+            if turn == 1:
+                early_k, early_v = key_gradient(s)
+                dk = (dk.astype(F32) + early_k).astype(BF16)
+                dv = (dv.astype(F32) + early_v).astype(BF16)
+            grad = grad + nt(dk, wa[1]) + nt(dv, wa[2])
             first = jnp.where(place_ref[LOCAL * turn + s] == 0, grad, 0.0)
             sums[FIRST_MEMORY : FIRST_MEMORY + THIN, :] += first
         return grad
 
     @pl.when(y == 1)
     def _():
+        for copy in reads:
+            copy.wait()
         left[...] = slots(1, None)
         handed.start()
-
-    for copy in rows_in:
-        copy.wait()
-    for s in range(LOCAL):
-        df[s, 0:THIN] = jnp.where(memory_row, thin_d[s, 0], df[s, 0:THIN])
-        hid[s, 0:THIN] = jnp.where(memory_row, thin_d[s, 1], hid[s, 0:THIN])
-    chunks = FF // CHUNK
-    stores = [
-        pltpu.make_async_copy(
-            staged.at[i % 2], terms_ref.at[:, pl.ds(CHUNK * i, CHUNK)], sem_stage.at[i % 2]
-        )
-        for i in range(chunks)
-    ]
-    for i in range(chunks):
-        for copy in chunk_reads(i):
-            copy.wait()
-        lanes = slice(CHUNK * i, CHUNK * (i + 1))
-        for s in range(LOCAL):
-            for j, buf in ((1, gb), (0, dub)):
-                old = buf[i % 2, s, 0:THIN]
-                buf[i % 2, s, 0:THIN] = jnp.where(memory_row, thin_f[s, j, :, lanes], old)
-        if i >= 2:
-            stores[i - 2].wait()
-        for j, (buf, rows) in enumerate(((dub, hid), (gb, df))):
-            terms = tn(
-                buf[i % 2].reshape(LOCAL * SEG, CHUNK), rows[...].reshape(LOCAL * SEG, D)
-            )
-            staged[i % 2, j] = terms.astype(BF16)
-        stores[i].start()
-        if i + 2 < chunks:
-            for copy in chunk_reads(i + 2):
-                copy.start()
+        lax.fori_loop(0, pairs, attend_at, 0)
 
     @pl.when(y == 0)
     def _():
+        for copy in reads:
+            copy.wait()
+        lax.fori_loop(0, pairs, attend_at, 0)
         handed.wait_recv()
         slots(0, given[...])
 
-    @pl.when(y == 1)
-    def _():
-        handed.wait_send()
-
     writes = [
-        pltpu.make_async_copy(dkb, dk_ref, sem_out.at[0]),
-        pltpu.make_async_copy(dvb, dv_ref, sem_out.at[1]),
-        pltpu.make_async_copy(thin_d, thin_d_ref, sem_out.at[2]),
-        pltpu.make_async_copy(thin_f, thin_f_ref, sem_out.at[3]),
-        pltpu.make_async_copy(sums, sums_ref, sem_out.at[4]),
+        pltpu.make_async_copy(dqb, dq_ref, sem_out.at[0]),
+        pltpu.make_async_copy(dkb, dk_ref, sem_out.at[1]),
+        pltpu.make_async_copy(dvb, dv_ref, sem_out.at[2]),
+        pltpu.make_async_copy(sums, sums_ref, sem_out.at[3]),
         *[
             pltpu.make_async_copy(tiles.at[i], first_rows(ref), sem_out.at[5 + i])
             for i, ref in enumerate(merged)
@@ -1406,9 +1412,59 @@
     ]
     for copy in writes:
         copy.start()
-    for copy in writes + stores[-2:]:
+
+    for copy in rows_in:
         copy.wait()
-    swap.wait()
+    for s in range(LOCAL):
+        df[s, 0:THIN] = jnp.where(memory_row, thin_d[s, 0], df[s, 0:THIN])
+        hid[s, 0:THIN] = jnp.where(memory_row, thin_d[s, 1], hid[s, 0:THIN])
+    chunks = FF // CHUNK
+
+    def store(i):
+        lanes = pl.ds(pl.multiple_of(CHUNK * i, CHUNK), CHUNK)
+        slot = lax.rem(i, 2)
+        return pltpu.make_async_copy(
+            staged.at[slot], terms_ref.at[:, lanes], sem_stage.at[slot]
+        )
+
+    def chunk(i, carry):
+        slot = lax.rem(i, 2)
+        for copy in chunk_reads(i):
+            copy.wait()
+        lanes = pl.ds(pl.multiple_of(CHUNK * i, CHUNK), CHUNK)
+        for s in range(LOCAL):
+            for j, buf in ((1, gb), (0, dub)):
+                old = buf[slot, s, 0:THIN]
+                buf[slot, s, 0:THIN] = jnp.where(memory_row, thin_f[s, j, :, lanes], old)
+
+        @pl.when(i >= 2)
+        def _():
+            store(i - 2).wait()
+
+        for j, (buf, rows) in enumerate(((dub, hid), (gb, df))):
+            terms = tn(
+                buf[slot].reshape(LOCAL * SEG, CHUNK), rows[...].reshape(LOCAL * SEG, D)
+            )
+            staged[slot, j] = terms.astype(BF16)
+        store(i).start()
+
+        @pl.when(i + 2 < chunks)
+        def _():
+            for copy in chunk_reads(i + 2):
+                copy.start()
+
+        return carry
+
+    lax.fori_loop(0, chunks, chunk, 0)
+
+    @pl.when(y == 1)
+    def _():
+        handed.wait_send()
+
+    for copy in [*writes, store(chunks - 2), store(chunks - 1)]:
+        copy.wait()
+    for copy in swap:
+        copy.wait()
 
 
 THIN_SHAPES = (
@@ -1418,28 +1474,27 @@
 )
 
 
-def chain_back(place, table, attn, ffn, q, k, v, saved, g, du, df, h, send, dk, dv, da, dq, c):
+def chain_back(place, table, attn, ffn, q, k, v, saved, g, du, df, h, halves, dc, logs, da, c):
     whole = sds((LOCAL, SEG, D), BF16)
     rows = pltpu.VMEM(whole.shape, BF16)
-    tile = pltpu.VMEM((LOCAL, THIN, D), BF16)
     dma = lambda *shape: pltpu.SemaphoreType.DMA(shape)
     outs = pl.pallas_call(
         chain_back_kernel,
         in_specs=[SMEM, VMEM] + [ANY] * 18,
-        out_specs=[ANY] * 10,
+        out_specs=[ANY] * 8,
         out_shape=[whole] * 5
-        + list(THIN_SHAPES)
-        + [sds((2, FF, D), BF16), sds(send.shape, BF16)],
-        input_output_aliases={15 + i: i for i in range(5)},
+        + [THIN_SHAPES[2]]
+        + [sds((2, FF, D), BF16), sds((2 * LOCAL, *halves[0].shape[1:]), BF16)],
+        input_output_aliases={18: 0, 19: 1},
         scratch_shapes=[
             pltpu.VMEM((4, D, D), BF16),
             pltpu.VMEM((2, FF, D), BF16),
-            tile,
+            *[rows] * 5,
+            pltpu.VMEM(logs.shape, F32),
             rows,
             rows,
             rows,
-            rows,
-            pltpu.VMEM((3, LOCAL, THIN, D), BF16),
+            pltpu.VMEM((2, LOCAL, THIN, D), BF16),
             rows,
             rows,
             pltpu.VMEM((2, LOCAL, SEG, CHUNK), BF16),
@@ -1455,12 +1510,12 @@
             dma(8),
             dma(2),
             dma(2),
-            dma(2),
+            dma(3),
         ],
         name="chain_back",
         compiler_params=params(collective_id=3, has_side_effects=True),
-    )(place, table, attn, ffn, q, k, v, *saved, g, du, df, h, send, dk, dv, da, dq, c)
-    return outs[:5], outs[5:8], outs[8], outs[9]
+    )(place, table, attn, ffn, q, k, v, *saved, g, du, df, h, *halves, dc, logs, da, c)
+    return outs
 
 
 def table_row(ref, index, entries):
@@ -1696,32 +1751,395 @@
     )(x, da, dq, dk, dv, c, sums, thin_sums)
 
 
-def add_thin_kernel(thin_f_ref, thin_d_ref, terms_ref, out_ref):
-    out_ref[...] = terms_ref[...]
-
-    @pl.when(lax.axis_index("tensor") == 0)
-    def _():
-        for j, (a, b) in enumerate(((0, 1), (1, 0))):
-            left = jnp.concatenate([thin_f_ref[s, a] for s in range(LOCAL)], axis=0)
-            right = jnp.concatenate([thin_d_ref[s, b] for s in range(LOCAL)], axis=0)
-            out_ref[j] = (terms_ref[j].astype(F32) + tn(left, right)).astype(BF16)
-
-
-def add_thin(terms, thin_d, thin_f):
-    block = pl.BlockSpec((2, CHUNK, D), lambda i: (0, i, 0))
+def scatter_steps(nz, place, lead, z_second, pieces, send_sem, recv_sem):
+    z, x, c, y = place
+    first, second, both = partners(place, lead)
+    to_first = device(z, first[0], c, first[1])
+    to_second = device(z, second[0], c, second[1])
+    to_core = device(z, x, 1 - c, y)
+    f_first, f_second = 2 - lead, 1 + lead
+
+    def at(f):
+        fx, fy = f // 2, f % 2
+        return x + fx * (1 - 2 * x), y + fy * (1 - 2 * y)
+
+    def term(piece, zz, core, f):
+        xx, yy = at(f)
+        return piece[2](piece[1], zz, xx, core, yy)
+
+    def copies(kind, zz, target, src, dst):
+        return [
+            remote(src(p), dst(p), send_sem.at[kind, zz, p[0]], recv_sem.at[kind, zz, p[0]], target)
+            for p in pieces
+        ]
+
+    def core_copies(zz, f):
+        return copies(
+            f, zz, to_core, lambda p: term(p, zz, 1 - c, f), lambda p: p[3].at[zz, f]
+        )
+
+    def second_copies(zz, across):
+        f = 3 if across else f_second
+        return copies(
+            4 + across, zz, to_second, lambda p: p[3].at[zz, f], lambda p: p[4].at[zz, across]
+        )
+
+    def first_copies(zz):
+        slot = 0 if z_second else zz
+        return copies(6, zz, to_first, lambda p: p[4].at[zz, 1], lambda p: p[5].at[slot])
+
+    def partial(p, zz, f):
+        return p[4].at[zz, f] if z_second else p[5].at[zz]
+
+    def beside(p, above, zz, f):
+        return p[6 + above].at[zz, f] if z_second else p[6 + above].at[zz]
+
+    def up_copies(zz, f):
+        return copies(
+            7 + 2 * f,
+            zz,
+            device(z + 1, x, c, y),
+            lambda p: partial(p, zz, f),
+            lambda p: beside(p, 0, zz, f),
+        )
+
+    def down_copies(zz, f):
+        return copies(
+            8 + 2 * f,
+            zz,
+            device(z - 1, x, c, y),
+            lambda p: partial(p, zz, f),
+            lambda p: beside(p, 1, zz, f),
+        )
+
+    def run(group, what):
+        for copy in group:
+            getattr(copy, what)()
+
+    def add(into, other):
+        for p in pieces:
+            a, b = into(p), other(p)
+            a[...] = (a[...].astype(F32) + b[...].astype(F32)).astype(a.dtype)
+
+    def turn(k):
+        upper = z // (nz // 2)
+        return (1 - upper) * (nz - 1 - k) + upper * k
+
+    def start(zz):
+        for f in (3, 1, 2, 0):
+            run(core_copies(zz, f), "start")
+
+    def stage0(zz):
+        for f in (3, 1, 2, 0):
+            run(core_copies(zz, f), "wait_recv")
+            add(lambda p: p[3].at[zz, f], lambda p: term(p, zz, c, f))
+        run(second_copies(zz, 1), "start")
+        run(second_copies(zz, 0), "start")
+
+    def from_below(zz, f):
+        run(up_copies(zz, f), "wait_recv")
+        add(lambda p: partial(p, zz, f), lambda p: beside(p, 0, zz, f))
+
+    def from_above(zz, f):
+        run(down_copies(zz, f), "wait_recv")
+        add(lambda p: partial(p, zz, f), lambda p: beside(p, 1, zz, f))
+
+    def along(zz, f):
+        @pl.when(zz > z)
+        def _():
+            @pl.when(z > 0)
+            def _():
+                from_below(zz, f)
+
+            run(up_copies(zz, f), "start")
+
+        @pl.when(zz < z)
+        def _():
+            @pl.when(z < nz - 1)
+            def _():
+                from_above(zz, f)
+
+            run(down_copies(zz, f), "start")
+
+    def stage1(zz):
+        run(second_copies(zz, 1), "wait_recv")
+        add(lambda p: p[4].at[zz, 1], lambda p: p[3].at[zz, f_first])
+        if z_second:
+            along(zz, 1)
+        else:
+            run(first_copies(zz), "start")
+
+    def stage2(zz):
+        run(second_copies(zz, 0), "wait_recv")
+        add(lambda p: p[4].at[zz, 0], lambda p: p[3].at[zz, 0])
+        if not z_second:
+            run(first_copies(zz), "wait_recv")
+            add(lambda p: p[5].at[zz], lambda p: p[4].at[zz, 0])
+        along(zz, 0)
+
+    def staged(stage):
+        return lambda k: stage(turn(k))
+
+    def at_owner(f):
+        @pl.when(z > 0)
+        def _():
+            from_below(z, f)
+
+        @pl.when(z < nz - 1)
+        def _():
+            from_above(z, f)
+
+    def end(outs):
+        if z_second:
+            at_owner(1)
+            run(first_copies(z), "start")
+        at_owner(0)
+        if z_second:
+            run(first_copies(z), "wait_recv")
+            add(lambda p: p[4].at[z, 0], lambda p: p[5].at[0])
+        for p, out in zip(pieces, outs):
+            out[...] = partial(p, z, 0)[...]
+
+    def sent(zz, carry):
+        for f in range(4):
+            run(core_copies(zz, f), "wait_send")
+        run(second_copies(zz, 1), "wait_send")
+        run(second_copies(zz, 0), "wait_send")
+        for f in range(2 if z_second else 1):
+
+            @pl.when(zz > z)
+            def _():
+                run(up_copies(zz, f), "wait_send")
+
+            @pl.when(zz < z)
+            def _():
+                run(down_copies(zz, f), "wait_send")
+
+        if z_second:
+
+            @pl.when(zz == z)
+            def _():
+                run(first_copies(zz), "wait_send")
+
+        else:
+            run(first_copies(zz), "wait_send")
+        return carry
+
+    stages = [staged(stage) for stage in (stage0, stage1, stage2)]
+    return start, stages, turn, end, lambda: lax.fori_loop(0, nz, sent, 0)
+
+
+def scatter_places(nz, shape, z_second):
+    lead = (nz, 2) if z_second else (nz,)
+    return [
+        pltpu.VMEM((nz, 4, *shape), BF16),
+        pltpu.VMEM((nz, 2, *shape), BF16),
+        pltpu.VMEM((1 if z_second else nz, *shape), BF16),
+        pltpu.VMEM((*lead, *shape), BF16),
+        pltpu.VMEM((*lead, *shape), BF16),
+    ]
+
+
+VEC_ROWS = FIRST_MEMORY + THIN
+
+
+def tail_kernel(nz, *refs):
+    (
+        place_ref,
+        sums_ref,
+        thin_sums_ref,
+        ffn_terms,
+        *rows_refs,
+        w_ref,
+        attn_out,
+        ffn_out,
+        vec_out,
+        grad_ref,
+        terms_f,
+        terms_a,
+        rows,
+        wb,
+        keep,
+        send,
+    ) = refs[:21]
+    places = [refs[21 + 5 * i : 26 + 5 * i] for i in range(3)]
+    vec_mine, vec_given, vec_z, send_sem, recv_sem, block_sem, in_sem, swap_sem, vec_sem = refs[36:]
+    place = z, x, c, y = my_place()
+    blocks = lambda zz: pltpu.make_async_copy(
+        ffn_terms.at[:, zz], terms_f.at[:, zz], block_sem.at[zz]
+    )
+    rows_in = [
+        pltpu.make_async_copy(src, rows.at[i], in_sem.at[2 + i]) for i, src in enumerate(rows_refs)
+    ]
+    rows_in.append(pltpu.make_async_copy(w_ref.at[pl.ds(0, 3)], wb, in_sem.at[8]))
+    steps = functools.partial(scatter_steps, nz, place, send_sem=send_sem, recv_sem=recv_sem)
+    up = steps(c, False, [(0, terms_f.at[0], hidden_view, *places[0])])
+    down = steps(1 - c, True, [(1, terms_f.at[1], hidden_view, *places[1])])
+    attn = steps(1 - c, True, [(2, terms_a, attn_view, *places[2])])
+    turn = up[2]
+    for k in range(nz):
+        blocks(turn(k)).start()
+    for copy in rows_in:
+        copy.start()
+
+    barrier = pltpu.get_barrier_semaphore()
+    others = [device(lax.rem(z + dz, nz), x, c, y) for dz in range(1, nz)]
+    for other in [device(z, 1 - x, c, y), device(z, x, 1 - c, y), device(z, x, c, 1 - y), *others]:
+        pl.semaphore_signal(
+            barrier, inc=1, device_id=other, device_id_type=pl.DeviceIdType.MESH
+        )
+    pl.semaphore_wait(barrier, 2 + nz)
+
+    def begin(k, carry):
+        zz = turn(k)
+        blocks(zz).wait()
+        up[0](zz)
+        down[0](zz)
+        return carry
+
+    def attn_terms(i, carry):
+        left, right = rows[i // 3], rows[i + 2]
+        value = tn(left.reshape(LOCAL * SEG, D), right.reshape(LOCAL * SEG, D))
+        terms_a[i] = value.astype(BF16).reshape(terms_a.shape[1:])
+        return carry
+
+    def token_rows(s):
+        total = rows[1, s].astype(F32)
+        for i in range(3):
+            total = total + nt(rows[2 + i, s], wb[i])
+        live = place_ref[LOCAL * y + s] >= 0
+        stay, go = split_rows(y, jnp.where(live, total, 0.0))
+        keep[s] = stay.astype(BF16)
+        send[s] = go.astype(BF16)
+
+    def vec_copies(phase):
+        if phase < 3:
+            target = (device(z, x, 1 - c, y), device(z, x, c, 1 - y), device(z, 1 - x, c, y))[phase]
+            sems = vec_sem.at[0, phase], vec_sem.at[1, phase]
+            return [remote(vec_mine.at[phase], vec_given.at[phase], *sems, target)]
+        return [
+            remote(
+                vec_mine.at[3], vec_z.at[dz], vec_sem.at[0, 3 + dz], vec_sem.at[1, 3 + dz], target
+            )
+            for dz, target in enumerate(others)
+        ]
+
+    def vec_start(phase):
+        if phase == 0:
+            vec_mine[0] = thin_sums_ref[...]
+            vec_mine[0, 0:FIRST_MEMORY] = (
+                thin_sums_ref[0:FIRST_MEMORY] + sums_ref[0:FIRST_MEMORY]
+            )
+            for r, i in ((QUERY_BIAS, 2), (VALUE_BIAS, 4)):
+                total = row_sum(rows[i].reshape(LOCAL * SEG, D).astype(F32))
+                vec_mine[0, r : r + 1] = total
+        else:
+            for copy in vec_copies(phase - 1):
+                copy.wait_recv()
+            vec_mine[phase] = vec_mine[phase - 1] + vec_given[phase - 1]
+        for copy in vec_copies(phase):
+            copy.start()
+
+    swap = place_rows(place, keep, send, grad_ref, swap_sem)
+
+    def stage(i, *groups):
+        for k in groups[-1]:
+            for group in groups[:-1]:
+                group[1][i](k)
+
+    def step(k, *groups):
+        for lag in range(3):
+            if 0 <= k - lag < nz:
+                stage(lag, *groups, (k - lag,))
+
+    lax.fori_loop(0, 1, begin, 0)
+    for k in range(nz):
+        if k + 1 < nz:
+            lax.fori_loop(k + 1, k + 2, begin, 0)
+        step(k, up, down)
+        if k == 0:
+            for copy in rows_in:
+                copy.wait()
+        if k < 2:
+            lax.fori_loop(2 * k, 2 * k + 2, attn_terms, 0)
+        if k == 1:
+            vec_start(0)
+        if k == 2:
+            token_rows(0)
+            vec_start(1)
+        if k == 3:
+            token_rows(1)
+        if k >= 1:
+            attn[0](turn(k - 1))
+        if k >= 2:
+            step(k - 2, attn)
+    for copy in swap:
+        copy.start()
+    attn[0](turn(nz - 1))
+    step(nz, up, down)
+    vec_start(2)
+    step(2, attn)
+    step(nz + 1, up, down)
+    vec_start(3)
+    step(3, attn)
+    up[3]([ffn_out.at[0]])
+    step(4, attn)
+    down[3]([ffn_out.at[1]])
+    step(5, attn)
+    attn[3]([attn_out])
+    total = vec_mine[3]
+    for dz, copy in enumerate(vec_copies(3)):
+        copy.wait_recv()
+        total = total + vec_z[dz]
+    vec_out[...] = total
+    for phase in range(4):
+        for copy in vec_copies(phase):
+            copy.wait_send()
+    for group in (up, down, attn):
+        group[4]()
+    for copy in swap:
+        copy.wait()
+
+
+def tail(place, sums, thin_sums, ffn_terms, x, da, dq, dk, dv, c, attn, shapes):
+    nz = lax.axis_size("dp") // 4
+    rows, hidden, half = shapes
+    attn_shape, ffn_shape = (4, nz, 2, 2, rows, D), (2, nz, 2, 2, 2, hidden, D)
+    part = pltpu.VMEM((LOCAL, half, D), BF16)
+    dma = lambda *shape: pltpu.SemaphoreType.DMA(shape)
     return pl.pallas_call(
-        add_thin_kernel,
-        grid=(FF // CHUNK,),
-        in_specs=[
-            pl.BlockSpec((LOCAL, 2, THIN, CHUNK), lambda i: (0, 0, 0, i)),
-            once(thin_d.shape, (0, 0, 0, 0)),
-            block,
+        functools.partial(tail_kernel, nz),
+        in_specs=[SMEM, VMEM, VMEM] + [ANY] * 8,
+        out_specs=[VMEM] * 3 + [ANY],
+        out_shape=[
+            sds((4, rows, HALF), BF16),
+            sds((2, hidden, D), BF16),
+            sds((VEC_ROWS, D), F32),
+            sds((2 * LOCAL, half, D), BF16),
         ],
-        out_specs=block,
-        out_shape=sds((2, FF, D), BF16),
-        name="add_thin",
-        compiler_params=params(),
-    )(thin_f, thin_d, terms)
+        scratch_shapes=[
+            pltpu.VMEM(ffn_shape, BF16),
+            pltpu.VMEM(attn_shape, BF16),
+            pltpu.VMEM((6, LOCAL, SEG, D), BF16),
+            pltpu.VMEM((3, D, D), BF16),
+            part,
+            part,
+            *scatter_places(nz, (hidden, D), False),
+            *scatter_places(nz, (hidden, D), True),
+            *scatter_places(nz, (4, rows, HALF), True),
+            pltpu.VMEM((4, VEC_ROWS, D), F32),
+            pltpu.VMEM((3, VEC_ROWS, D), F32),
+            pltpu.VMEM((nz - 1, VEC_ROWS, D), F32),
+            dma(11, nz, 3),
+            dma(11, nz, 3),
+            dma(nz),
+            dma(9),
+            dma(3),
+            dma(2, 2 + nz),
+        ],
+        name="tail",
+        compiler_params=params(62, collective_id=1, has_side_effects=True),
+    )(place, sums, thin_sums, ffn_terms.reshape(ffn_shape), x, da, dq, dk, dv, c, attn)
 
 
 def update(gradient, momentum, weight, average, rate, grad_scale):
@@ -1833,25 +2251,28 @@
     keep, send, h, g, du, df, da, dc, c, log_total, sums = rows_part(
         place, x, q, k, v, c, log_tokens, cotangent, cot_other, attn, ffn, table
     )
-    dq, dk, dv = attend_back(q, k, v, dc, log_total)
-    (dk, dv, da, dq, c), thin, ffn_terms, received = chain_back(
-        place, table, attn, ffn, q, k, v, saved, g, du, df, h, send, dk, dv, da, dq, c
+    da, c, dq, dk, dv, thin_sums, ffn_terms, activations = chain_back(
+        place, table, attn, ffn, q, k, v, saved, g, du, df, h, (keep, send), dc, log_total, da, c
     )
-    thin_d, thin_f, thin_sums = thin
-    activations = joined(keep, received)
-
-    keep, send = token_gradient(place, da, dq, dk, dv, attn)
-    token_grad = joined(keep, swap(send))
-    ffn_terms = add_thin(ffn_terms, thin_d, thin_f)
-    attn_terms, vec_terms = attn_gradient(x, da, dq, dk, dv, c, sums, thin_sums)
-    vec_terms = vec_terms[:NVEC]
-
-    attn_grad, ffn_grad, vec_grad = scatter_gradients(
-        attn_terms,
-        ffn_terms,
-        vec_terms,
-        (attention.shape[1], feedforward.shape[2], vectors.shape[0]),
-    )
+    rows, hidden, entries = attention.shape[1], feedforward.shape[2], vectors.shape[0]
+    if rows % THIN == 0:
+        shapes = (rows, hidden, tokens.shape[1])
+        attn_grad, ffn_grad, vec_sums, token_grad = tail(
+            place, sums, thin_sums, ffn_terms, x, da, dq, dk, dv, c, attn, shapes
+        )
+        attn_grad = attn_grad.astype(F32)
+        ffn_grad = jnp.swapaxes(ffn_grad, 1, 2).astype(F32)
+        index = lax.axis_index("dp") * 2 + lax.axis_index("tensor")
+        vec_grad = lax.dynamic_slice_in_dim(
+            vec_sums[:NVEC].reshape(-1), index * entries, entries
+        )
+    else:
+        keep, send = token_gradient(place, da, dq, dk, dv, attn)
+        token_grad = joined(keep, swap(send))
+        attn_terms, vec_terms = attn_gradient(x, da, dq, dk, dv, c, sums, thin_sums)
+        attn_grad, ffn_grad, vec_grad = scatter_gradients(
+            attn_terms, ffn_terms, vec_terms[:NVEC], (rows, hidden, entries)
+        )
     grad_scale = 1.0 / math.sqrt(lax.axis_size("dp") * SLOTS * ROWS)
     attn_new = update(attn_grad, attn_momentum, attention, attn_average, ATTENTION_RATE, grad_scale)
     ffn_new = update(ffn_grad, ffn_momentum, feedforward, ffn_average, FEEDFORWARD_RATE, grad_scale)

time: 352 us -> 321 us (0.912)
  Pallas kernels: 319 us -> 299 us
  local copies, waits for them, and re-layouts: 15.6 us -> 10.7 us
  other arithmetic: 10.6 us -> 6.36 us
    pallas_call x7 -> x1, Pallas kernels: 127 us -> 91.6 us  [tail(): pl.pallas_call(functools.partial(tail_kernel, nz), in_specs=[SMEM, VMEM,...]
    pallas_call x1, Pallas kernels: 40.2 us -> 55 us  [chain_back(): pl.pallas_call(chain_back_kernel, in_specs=[SMEM, VMEM] + [ANY] * 18, out...]
    unnamed x27 -> x31, local copies, waits for them, and re-layouts: 10.9 us -> 9.93 us
  transfers between devices with their start and end apart: 1 -> 0, of which waited for: 0 -> 0; matrix products, arithmetic and copies ran while one was open for 3% -> 0% of each run, Pallas kernels for 27% -> 0%
where the time goes in v1:
time: 321 us; the launch traced here: 317 us
  Pallas kernels  299 us (93%)
  local copies, waits for them, and re-layouts  10.7 us (3%)
  other arithmetic  6.36 us (2%)
    pallas_call x1, Pallas kernels, tail(): pl.pallas_call(functools.partial(tail_kernel, nz), in_specs=[SMEM, VMEM,...  91.6 us
    pallas_call x1, Pallas kernels, head(): pl.pallas_call(functools.partial(head_kernel, nz, entries), in_specs=[ANY...  74.6 us
    pallas_call x1, Pallas kernels, rows_part(): pl.pallas_call(rows_kernel, grid=(LOCAL,), in_specs=[SMEM, rows, rows, th...  58 us
    pallas_call x1, Pallas kernels, chain_back(): pl.pallas_call(chain_back_kernel, in_specs=[SMEM, VMEM] + [ANY] * 18, out...  55 us
    pallas_call x1, Pallas kernels, chain(): pl.pallas_call(chain_kernel, in_specs=[SMEM, VMEM] + [ANY] * 7, out_specs...  19.6 us
    unnamed x31, local copies, waits for them, and re-layouts  9.93 us

profile of v1, /device:TPU:1, one launch (start us, length us, event | category | flops | bytes accessed | tf_op | source)
XLA Modules:
  0.0 316.9 jit_solution(9090721128042296733)
XLA Ops:
  0.6 0.0 copy-start
  0.7 0.0 copy-start.4
  0.7 0.0 copy-start.10
  0.7 2.9 copy.29.tokens
  3.5 0.0 copy-done
  3.5 0.7 convert_bitcast_fusion.ffn_src
  4.3 0.0 copy-done.4
  4.3 0.7 convert_element_type.19.attn_src
  5.0 0.6 bitcast_convert_fusion.vec_src
  5.6 74.6 %head.1 = (bf16[4,4,2,2,48,768]{5,4,3,2,1,0:T(8,128)(2,1)}, bf16[2,4,2,2,2,96,768]{6,5,4,3,2,1,0:T(8,128)(2,1)}, f32[4,2,2,2,8,128]{5,4,3,2,1,0:T(8,128)}, bf16[...) custom-call(bf16[4,48,384]{2,1,0:T(8,128)(2,1)} %convert_element_typ, ...), custom_call_target="tpu_custom_call" | custom-call | tf_op jit(solution)/shard_map/head/pallas_call | solution.py:1664
  80.2 0.9 copy.36
  81.2 0.7 reshape.48.table_ref
  81.9 1.4 copy.30.cot_ref.mine_ref
  83.3 19.6 %chain.1 = (bf16[2,512,768]{2,1,0:T(8,128)(2,1)}, bf16[2,512,768]{2,1,0:T(8,128)(2,1)}, bf16[2,512,768]{2,1,0:T(8,128)(2,1)}, bf16[2,512,768]{2,1,0:T(8,128)(2,1...) custom-call(s32[4]{0:T(128)} %refs_0_.1, ...), custom_call_target="tpu_custom_call", output_to_operand_aliasing={{0}: (4, {}), {1}: (5, {}), {2}: (6, {}), {3}: (7, {})} | custom-call | tf_op jit(solution)/shard_map/chain/pallas_call | solution.py:895
  102.9 58.0 %rows_part.1 = (bf16[2,251,768]{2,1,0:T(8,128)(2,1)}, bf16[2,251,768]{2,1,0:T(8,128)(2,1)}, bf16[2,512,768]{2,1,0:T(8,128)(2,1)}, bf16[2,512,3072]{2,1,0:T(8,128...) custom-call(s32[4]{0:T(128)} %refs_0_.1, ...), custom_call_target="tpu_custom_call" | custom-call | tf_op jit(solution)/shard_map/rows_part/pallas_call | solution.py:1129
  160.9 55.0 %chain_back.1 = (bf16[2,512,768]{2,1,0:T(8,128)(2,1)}, bf16[2,512,768]{2,1,0:T(8,128)(2,1)}, bf16[2,512,768]{2,1,0:T(8,128)(2,1)}, bf16[2,512,768]{2,1,0:T(8,128...) custom-call(s32[4]{0:T(128)} %refs_0_.1, ...), custom_call_target="tpu_custom_call", output_to_operand_aliasing={{0}: (18, {}), {1}: (19, {})} | custom-call | tf_op jit(solution)/shard_map/chain_back/pallas_call | solution.py:1481
  215.9 0.0 copy-start.5
  215.9 91.6 %tail.1 = (bf16[4,48,384]{2,1,0:T(8,128)(2,1)}, bf16[2,96,768]{2,1,0:T(8,128)(2,1)}, f32[28,768]{1,0:T(8,128)}, bf16[4,251,768]{2,1,0:T(8,128)(2,1)}) custom-call(s32[4]{0:T(128)} %refs_0_.1, f32[16,768]{1,0:T(8,128)} %get-tuple-element.79.refs_1_, f32[28,768]{1,0:T(8,128)} %get-tuple-element.80.refs_2_, bf16[2,4,2,2,2,96,768]{6,5,4,3,2,1,0:T(8,128)(2,1)} %bitcast.29, ...), custom_call_target="tpu_custom_call" | custom-call | tf_op jit(solution)/shard_map/tail/pallas_call | solution.py:2110
  307.6 2.7 multiply_add_fusion
  310.2 2.3 copy.33
  312.6 1.0 multiply_add_fusion.1
  313.7 0.7 multiply_add_fusion.2
  314.3 0.0 copy-done.1
  314.4 2.3 copy.32
  (23 shorter events, 0.1 us)
Async XLA Ops:
  0.6 2.9 copy-start
  0.7 3.6 %copy-start.4 = (f32[4,48,384]{2,1,0:T(8,128)S(1)}, f32[4,48,384]{2,1,0:T(8,128)}, u32[]{:S(2)}) copy-start(f32[4,48,384]{2,1,0:T(8,128)} %param.15) | copy-start | bytes 884740
  0.7 4.3 %copy-start.10 = (f32[528]{0:T(1024)S(1)}, f32[528]{0:T(1024)}, u32[]{:S(2)}) copy-start(f32[528]{0:T(1024)} %param.17) | copy-start | bytes 6340
  4.3 77.6 %copy-start.3 = (bf16[4,251,768]{2,0,1:T(4,128)(2,1)S(1)}, bf16[4,251,768]{2,0,1:T(4,128)(2,1)}, u32[]{:S(2)}) copy-start(bf16[4,251,768]{2,0,1:T(4,128)(2,1)} %param.14) | copy-start | bytes 4626436
  215.9 91.6 %copy-start.5 = (f32[2,768,96]{1,2,0:T(8,128)S(1)}, f32[2,768,96]{1,2,0:T(8,128)}, u32[]{:S(2)}) copy-start(f32[2,768,96]{1,2,0:T(8,128)} %param.22) | copy-start | bytes 1769476
  307.6 2.7 copy-start.2
  310.2 2.4 copy-start.6
  310.2 2.4 copy-start.7
  310.2 2.4 copy-start.8
  312.6 1.0 copy-start.9
  312.6 1.1 copy-start.11
  312.6 1.1 copy-start.12
  312.6 1.8 copy-start.1

commit v2 on v1

--- a/solution.py
+++ b/solution.py
@@ -1844,28 +1844,31 @@
         run(down_copies(zz, f), "wait_recv")
         add(lambda p: partial(p, zz, f), lambda p: beside(p, 1, zz, f))
 
+    def from_end(zz, f):
+        @pl.when((zz > z) & (z == 0))
+        def _():
+            run(up_copies(zz, f), "start")
+
+        @pl.when((zz < z) & (z == nz - 1))
+        def _():
+            run(down_copies(zz, f), "start")
+
     def along(zz, f):
-        @pl.when(zz > z)
+        @pl.when((zz > z) & (z > 0))
         def _():
-            @pl.when(z > 0)
-            def _():
-                from_below(zz, f)
-
+            from_below(zz, f)
             run(up_copies(zz, f), "start")
 
-        @pl.when(zz < z)
+        @pl.when((zz < z) & (z < nz - 1))
         def _():
-            @pl.when(z < nz - 1)
-            def _():
-                from_above(zz, f)
-
+            from_above(zz, f)
             run(down_copies(zz, f), "start")
 
     def stage1(zz):
         run(second_copies(zz, 1), "wait_recv")
         add(lambda p: p[4].at[zz, 1], lambda p: p[3].at[zz, f_first])
         if z_second:
-            along(zz, 1)
+            from_end(zz, 1)
         else:
             run(first_copies(zz), "start")
 
@@ -1875,6 +1878,11 @@
         if not z_second:
             run(first_copies(zz), "wait_recv")
             add(lambda p: p[5].at[zz], lambda p: p[4].at[zz, 0])
+        from_end(zz, 0)
+        if z_second:
+            along(zz, 1)
+
+    def stage3(zz):
         along(zz, 0)
 
     def staged(stage):
@@ -1925,7 +1933,7 @@
             run(first_copies(zz), "wait_send")
         return carry
 
-    stages = [staged(stage) for stage in (stage0, stage1, stage2)]
+    stages = [staged(stage) for stage in (stage0, stage1, stage2, stage3)]
     return start, stages, turn, end, lambda: lax.fori_loop(0, nz, sent, 0)
 
 
@@ -2048,44 +2056,45 @@
                 group[1][i](k)
 
     def step(k, *groups):
-        for lag in range(3):
+        for lag in range(4):
             if 0 <= k - lag < nz:
                 stage(lag, *groups, (k - lag,))
 
-    lax.fori_loop(0, 1, begin, 0)
-    for k in range(nz):
-        if k + 1 < nz:
-            lax.fori_loop(k + 1, k + 2, begin, 0)
-        step(k, up, down)
-        if k == 0:
-            for copy in rows_in:
-                copy.wait()
-        if k < 2:
-            lax.fori_loop(2 * k, 2 * k + 2, attn_terms, 0)
-        if k == 1:
-            vec_start(0)
-        if k == 2:
-            token_rows(0)
-            vec_start(1)
-        if k == 3:
-            token_rows(1)
-        if k >= 1:
-            attn[0](turn(k - 1))
-        if k >= 2:
-            step(k - 2, attn)
+    lax.fori_loop(0, 2, begin, 0)
+    step(0, up, down)
+    for copy in rows_in:
+        copy.wait()
+    lax.fori_loop(0, 2, attn_terms, 0)
+    lax.fori_loop(2, 3, begin, 0)
+    step(1, up, down)
+    lax.fori_loop(2, 4, attn_terms, 0)
+    vec_start(0)
+    lax.fori_loop(3, 4, begin, 0)
+    attn[0](turn(0))
+    step(2, up, down)
+    step(0, attn)
+    attn[0](turn(1))
+    token_rows(0)
+    vec_start(1)
+    step(3, up, down)
+    step(1, attn)
+    attn[0](turn(2))
+    token_rows(1)
     for copy in swap:
         copy.start()
-    attn[0](turn(nz - 1))
-    step(nz, up, down)
+    step(4, up, down)
+    step(2, attn)
+    attn[0](turn(3))
     vec_start(2)
-    step(2, attn)
-    step(nz + 1, up, down)
+    step(5, up, down)
+    step(3, attn)
     vec_start(3)
-    step(3, attn)
+    step(6, up, down)
+    step(4, attn)
     up[3]([ffn_out.at[0]])
-    step(4, attn)
+    step(5, attn)
     down[3]([ffn_out.at[1]])
-    step(5, attn)
+    step(6, attn)
     attn[3]([attn_out])
     total = vec_mine[3]
     for dz, copy in enumerate(vec_copies(3)):

time: 321 us -> 322 us (level)
  no operation moved by 1% of the time
where the time goes in v2:
time: 322 us; the launch traced here: 320 us
  Pallas kernels  302 us (94%)
  local copies, waits for them, and re-layouts  10.7 us (3%)
  other arithmetic  6.36 us (2%)
    pallas_call x1, Pallas kernels, tail(): pl.pallas_call(functools.partial(tail_kernel, nz), in_specs=[SMEM, VMEM,...  94.4 us
    pallas_call x1, Pallas kernels, head(): pl.pallas_call(functools.partial(head_kernel, nz, entries), in_specs=[ANY...  74.6 us
    pallas_call x1, Pallas kernels, rows_part(): pl.pallas_call(rows_kernel, grid=(LOCAL,), in_specs=[SMEM, rows, rows, th...  58 us
    pallas_call x1, Pallas kernels, chain_back(): pl.pallas_call(chain_back_kernel, in_specs=[SMEM, VMEM] + [ANY] * 18, out...  55 us
    pallas_call x1, Pallas kernels, chain(): pl.pallas_call(chain_kernel, in_specs=[SMEM, VMEM] + [ANY] * 7, out_specs...  19.6 us
    unnamed x31, local copies, waits for them, and re-layouts  9.93 us

profile of v2, /device:TPU:1, one launch (start us, length us, event | category | flops | bytes accessed | tf_op | source)
XLA Modules:
  0.0 319.7 jit_solution(3189083662975273109)
XLA Ops:
  0.7 2.9 copy.29.tokens
  3.5 0.0 copy-done
  3.5 0.7 convert_bitcast_fusion.ffn_src
  4.3 0.7 convert_element_type.19.attn_src
  5.0 0.0 copy-done.10
  5.0 0.6 bitcast_convert_fusion.vec_src
  5.6 74.6 %head.1 = (bf16[4,4,2,2,48,768]{5,4,3,2,1,0:T(8,128)(2,1)}, bf16[2,4,2,2,2,96,768]{6,5,4,3,2,1,0:T(8,128)(2,1)}, f32[4,2,2,2,8,128]{5,4,3,2,1,0:T(8,128)}, bf16[...) custom-call(bf16[4,48,384]{2,1,0:T(8,128)(2,1)} %convert_element_typ, ...), custom_call_target="tpu_custom_call" | custom-call | tf_op jit(solution)/shard_map/head/pallas_call | solution.py:1664
  80.2 0.9 copy.36
  81.2 0.7 reshape.48.table_ref
  81.9 0.0 copy-done.3
  81.9 1.4 copy.30.cot_ref.mine_ref
  83.3 19.6 %chain.1 = (bf16[2,512,768]{2,1,0:T(8,128)(2,1)}, bf16[2,512,768]{2,1,0:T(8,128)(2,1)}, bf16[2,512,768]{2,1,0:T(8,128)(2,1)}, bf16[2,512,768]{2,1,0:T(8,128)(2,1...) custom-call(s32[4]{0:T(128)} %refs_0_.1, ...), custom_call_target="tpu_custom_call", output_to_operand_aliasing={{0}: (4, {}), {1}: (5, {}), {2}: (6, {}), {3}: (7, {})} | custom-call | tf_op jit(solution)/shard_map/chain/pallas_call | solution.py:895
  102.9 58.0 %rows_part.1 = (bf16[2,251,768]{2,1,0:T(8,128)(2,1)}, bf16[2,251,768]{2,1,0:T(8,128)(2,1)}, bf16[2,512,768]{2,1,0:T(8,128)(2,1)}, bf16[2,512,3072]{2,1,0:T(8,128...) custom-call(s32[4]{0:T(128)} %refs_0_.1, ...), custom_call_target="tpu_custom_call" | custom-call | tf_op jit(solution)/shard_map/rows_part/pallas_call | solution.py:1129
  160.9 55.0 %chain_back.1 = (bf16[2,512,768]{2,1,0:T(8,128)(2,1)}, bf16[2,512,768]{2,1,0:T(8,128)(2,1)}, bf16[2,512,768]{2,1,0:T(8,128)(2,1)}, bf16[2,512,768]{2,1,0:T(8,128...) custom-call(s32[4]{0:T(128)} %refs_0_.1, ...), custom_call_target="tpu_custom_call", output_to_operand_aliasing={{0}: (18, {}), {1}: (19, {})} | custom-call | tf_op jit(solution)/shard_map/chain_back/pallas_call | solution.py:1481
  215.9 0.0 copy-start.5
  215.9 94.4 %tail.1 = (bf16[4,48,384]{2,1,0:T(8,128)(2,1)}, bf16[2,96,768]{2,1,0:T(8,128)(2,1)}, f32[28,768]{1,0:T(8,128)}, bf16[4,251,768]{2,1,0:T(8,128)(2,1)}) custom-call(s32[4]{0:T(128)} %refs_0_.1, f32[16,768]{1,0:T(8,128)} %get-tuple-element.79.refs_1_, f32[28,768]{1,0:T(8,128)} %get-tuple-element.80.refs_2_, bf16[2,4,2,2,2,96,768]{6,5,4,3,2,1,0:T(8,128)(2,1)} %bitcast.29, ...), custom_call_target="tpu_custom_call" | custom-call | tf_op jit(solution)/shard_map/tail/pallas_call | solution.py:2119
  310.3 2.7 multiply_add_fusion
  313.0 0.0 copy-done.2
  313.0 2.3 copy.33
  315.3 0.0 copy-done.6
  315.3 1.0 multiply_add_fusion.1
  316.4 0.7 multiply_add_fusion.2
  317.1 0.0 copy-done.1
  317.1 2.3 copy.32
  (23 shorter events, 0.1 us)
Async XLA Ops:
  0.6 2.9 copy-start
  0.7 3.6 %copy-start.4 = (f32[4,48,384]{2,1,0:T(8,128)S(1)}, f32[4,48,384]{2,1,0:T(8,128)}, u32[]{:S(2)}) copy-start(f32[4,48,384]{2,1,0:T(8,128)} %param.15) | copy-start | bytes 884740
  0.7 4.3 %copy-start.10 = (f32[528]{0:T(1024)S(1)}, f32[528]{0:T(1024)}, u32[]{:S(2)}) copy-start(f32[528]{0:T(1024)} %param.17) | copy-start | bytes 6340
  4.3 77.6 %copy-start.3 = (bf16[4,251,768]{2,0,1:T(4,128)(2,1)S(1)}, bf16[4,251,768]{2,0,1:T(4,128)(2,1)}, u32[]{:S(2)}) copy-start(bf16[4,251,768]{2,0,1:T(4,128)(2,1)} %param.14) | copy-start | bytes 4626436
  215.9 94.4 %copy-start.5 = (f32[2,768,96]{1,2,0:T(8,128)S(1)}, f32[2,768,96]{1,2,0:T(8,128)}, u32[]{:S(2)}) copy-start(f32[2,768,96]{1,2,0:T(8,128)} %param.22) | copy-start | bytes 1769476
  310.3 2.7 copy-start.2
  313.0 2.4 copy-start.6
  313.0 2.4 copy-start.7
  313.0 2.4 copy-start.8
  315.3 1.0 copy-start.9
  315.3 1.1 copy-start.11
  315.3 1.1 copy-start.12
  315.3 1.8 copy-start.1

commit v3 on v2

--- a/solution.py
+++ b/solution.py
@@ -1008,7 +1008,8 @@
             keys = slice(0, TILE * (part + 1))
             score = nt(own_lanes(k[keys], head), q[rows])
             share = jnp.exp(score - logs[head : head + 1, rows])
-            share = jnp.where(seen(score, TILE * part), share, 0.0)
+            diagonal = jnp.where(seen(share[rows], 0), share[rows], 0.0)
+            share = jnp.concatenate([share[: TILE * part], diagonal], axis=0) if part else diagonal
             share_grad = nt(own_lanes(v[keys], head), dc[rows])
             inner = jnp.sum(share_grad * share, axis=0, keepdims=True)
             score_grad = (share * (share_grad - inner)).astype(BF16)
@@ -1592,13 +1593,14 @@
     own[0].wait()
     own[1].wait()
     begin()
+    step(1)
     halves.start()
 
     def loop(t, carry):
         step(t)
         return carry
 
-    lax.fori_loop(1, nz + 2, loop, 0)
+    lax.fori_loop(2, nz + 2, loop, 0)
     own[2].wait()
     for begin2, _, _, _ in late:
         begin2()
@@ -1981,9 +1983,9 @@
     ]
     rows_in.append(pltpu.make_async_copy(w_ref.at[pl.ds(0, 3)], wb, in_sem.at[8]))
     steps = functools.partial(scatter_steps, nz, place, send_sem=send_sem, recv_sem=recv_sem)
-    up = steps(c, False, [(0, terms_f.at[0], hidden_view, *places[0])])
+    up = steps(c, True, [(0, terms_f.at[0], hidden_view, *places[0])])
     down = steps(1 - c, True, [(1, terms_f.at[1], hidden_view, *places[1])])
-    attn = steps(1 - c, True, [(2, terms_a, attn_view, *places[2])])
+    attn = steps(1, False, [(2, terms_a, attn_view, *places[2])])
     turn = up[2]
     for k in range(nz):
         blocks(turn(k)).start()
@@ -2133,9 +2135,9 @@
             pltpu.VMEM((3, D, D), BF16),
             part,
             part,
-            *scatter_places(nz, (hidden, D), False),
             *scatter_places(nz, (hidden, D), True),
-            *scatter_places(nz, (4, rows, HALF), True),
+            *scatter_places(nz, (hidden, D), True),
+            *scatter_places(nz, (4, rows, HALF), False),
             pltpu.VMEM((4, VEC_ROWS, D), F32),
             pltpu.VMEM((3, VEC_ROWS, D), F32),
             pltpu.VMEM((nz - 1, VEC_ROWS, D), F32),

time: 322 us -> 316 us (0.981)
  Pallas kernels: 302 us -> 294 us
    pallas_call x1, Pallas kernels: 94.4 us -> 87.1 us  [tail(): pl.pallas_call(functools.partial(tail_kernel, nz), in_specs=[SMEM, VMEM,...]
where the time goes in v3:
time: 316 us; the launch traced here: 312 us
  Pallas kernels  294 us (93%)
  local copies, waits for them, and re-layouts  10.7 us (3%)
  other arithmetic  6.36 us (2%)
    pallas_call x1, Pallas kernels, tail(): pl.pallas_call(functools.partial(tail_kernel, nz), in_specs=[SMEM, VMEM,...  87.1 us
    pallas_call x1, Pallas kernels, head(): pl.pallas_call(functools.partial(head_kernel, nz, entries), in_specs=[ANY...  74.6 us
    pallas_call x1, Pallas kernels, rows_part(): pl.pallas_call(rows_kernel, grid=(LOCAL,), in_specs=[SMEM, rows, rows, th...  58 us
    pallas_call x1, Pallas kernels, chain_back(): pl.pallas_call(chain_back_kernel, in_specs=[SMEM, VMEM] + [ANY] * 18, out...  55 us
    pallas_call x1, Pallas kernels, chain(): pl.pallas_call(chain_kernel, in_specs=[SMEM, VMEM] + [ANY] * 7, out_specs...  19.6 us
    unnamed x31, local copies, waits for them, and re-layouts  9.93 us

profile of v3, /device:TPU:1, one launch (start us, length us, event | category | flops | bytes accessed | tf_op | source)
XLA Modules:
  0.0 312.5 jit_solution(4951453083090669881)
XLA Ops:
  0.6 0.0 copy-start
  0.7 0.0 copy-start.4
  0.7 2.9 copy.29.tokens
  3.5 0.7 convert_bitcast_fusion.ffn_src
  4.3 0.7 convert_element_type.19.attn_src
  5.0 0.0 copy-done.10
  5.0 0.6 bitcast_convert_fusion.vec_src
  5.6 74.6 %head.1 = (bf16[4,4,2,2,48,768]{5,4,3,2,1,0:T(8,128)(2,1)}, bf16[2,4,2,2,2,96,768]{6,5,4,3,2,1,0:T(8,128)(2,1)}, f32[4,2,2,2,8,128]{5,4,3,2,1,0:T(8,128)}, bf16[...) custom-call(bf16[4,48,384]{2,1,0:T(8,128)(2,1)} %convert_element_typ, ...), custom_call_target="tpu_custom_call" | custom-call | tf_op jit(solution)/shard_map/head/pallas_call | solution.py:1666
  80.2 0.9 copy.36
  81.2 0.7 reshape.48.table_ref
  81.9 1.4 copy.30.cot_ref.mine_ref
  83.3 19.6 %chain.1 = (bf16[2,512,768]{2,1,0:T(8,128)(2,1)}, bf16[2,512,768]{2,1,0:T(8,128)(2,1)}, bf16[2,512,768]{2,1,0:T(8,128)(2,1)}, bf16[2,512,768]{2,1,0:T(8,128)(2,1...) custom-call(s32[4]{0:T(128)} %refs_0_.1, ...), custom_call_target="tpu_custom_call", output_to_operand_aliasing={{0}: (4, {}), {1}: (5, {}), {2}: (6, {}), {3}: (7, {})} | custom-call | tf_op jit(solution)/shard_map/chain/pallas_call | solution.py:895
  102.9 58.0 %rows_part.1 = (bf16[2,251,768]{2,1,0:T(8,128)(2,1)}, bf16[2,251,768]{2,1,0:T(8,128)(2,1)}, bf16[2,512,768]{2,1,0:T(8,128)(2,1)}, bf16[2,512,3072]{2,1,0:T(8,128...) custom-call(s32[4]{0:T(128)} %refs_0_.1, ...), custom_call_target="tpu_custom_call" | custom-call | tf_op jit(solution)/shard_map/rows_part/pallas_call | solution.py:1130
  160.9 55.0 %chain_back.1 = (bf16[2,512,768]{2,1,0:T(8,128)(2,1)}, bf16[2,512,768]{2,1,0:T(8,128)(2,1)}, bf16[2,512,768]{2,1,0:T(8,128)(2,1)}, bf16[2,512,768]{2,1,0:T(8,128...) custom-call(s32[4]{0:T(128)} %refs_0_.1, ...), custom_call_target="tpu_custom_call", output_to_operand_aliasing={{0}: (18, {}), {1}: (19, {})} | custom-call | tf_op jit(solution)/shard_map/chain_back/pallas_call | solution.py:1482
  215.9 0.0 copy-start.5
  215.9 87.1 %tail.1 = (bf16[4,48,384]{2,1,0:T(8,128)(2,1)}, bf16[2,96,768]{2,1,0:T(8,128)(2,1)}, f32[28,768]{1,0:T(8,128)}, bf16[4,251,768]{2,1,0:T(8,128)(2,1)}) custom-call(s32[4]{0:T(128)} %refs_0_.1, f32[16,768]{1,0:T(8,128)} %get-tuple-element.79.refs_1_, f32[28,768]{1,0:T(8,128)} %get-tuple-element.80.refs_2_, bf16[2,4,2,2,2,96,768]{6,5,4,3,2,1,0:T(8,128)(2,1)} %bitcast.29, ...), custom_call_target="tpu_custom_call" | custom-call | tf_op jit(solution)/shard_map/tail/pallas_call | solution.py:2121
  303.1 2.7 multiply_add_fusion
  305.8 2.3 copy.33
  308.1 1.0 multiply_add_fusion.1
  309.2 0.0 copy-done.11
  309.2 0.0 copy-done.12
  309.2 0.7 multiply_add_fusion.2
  309.9 0.0 copy-done.1
  309.9 2.3 copy.32
  (23 shorter events, 0.1 us)
Async XLA Ops:
  0.6 2.9 copy-start
  0.7 3.6 %copy-start.4 = (f32[4,48,384]{2,1,0:T(8,128)S(1)}, f32[4,48,384]{2,1,0:T(8,128)}, u32[]{:S(2)}) copy-start(f32[4,48,384]{2,1,0:T(8,128)} %param.15) | copy-start | bytes 884740
  0.7 4.3 %copy-start.10 = (f32[528]{0:T(1024)S(1)}, f32[528]{0:T(1024)}, u32[]{:S(2)}) copy-start(f32[528]{0:T(1024)} %param.17) | copy-start | bytes 6340
  4.3 77.6 %copy-start.3 = (bf16[4,251,768]{2,0,1:T(4,128)(2,1)S(1)}, bf16[4,251,768]{2,0,1:T(4,128)(2,1)}, u32[]{:S(2)}) copy-start(bf16[4,251,768]{2,0,1:T(4,128)(2,1)} %param.14) | copy-start | bytes 4626436
  215.9 87.2 %copy-start.5 = (f32[2,768,96]{1,2,0:T(8,128)S(1)}, f32[2,768,96]{1,2,0:T(8,128)}, u32[]{:S(2)}) copy-start(f32[2,768,96]{1,2,0:T(8,128)} %param.22) | copy-start | bytes 1769476
  303.1 2.7 copy-start.2
  305.7 2.4 copy-start.6
  305.7 2.4 copy-start.7
  305.8 2.4 copy-start.8
  308.1 1.0 copy-start.9
  308.1 1.1 copy-start.11
  308.1 1.1 copy-start.12
  308.1 1.8 copy-start.1

commit v4 on v3

--- a/solution.py
+++ b/solution.py
@@ -1548,7 +1548,7 @@
     tokens,
     attn_ref,
     ffn_ref,
-    vec_ref,
+    table_ref,
     x_ref,
     q_ref,
     k_ref,
@@ -1557,6 +1557,7 @@
     log_ref,
     wa,
     vec,
+    table,
     mine,
     other,
     xb,
@@ -1607,9 +1608,11 @@
     own[3].wait()
     halves.wait()
     end_arrive()
+    for index in range(NVEC):
+        table[index : index + 1] = table_row(vec, index, entries)
     outs = [
         pltpu.make_async_copy(wa, attn_ref, out_sem.at[0]),
-        pltpu.make_async_copy(vec, vec_ref, out_sem.at[1]),
+        pltpu.make_async_copy(table, table_ref, out_sem.at[1]),
     ]
     for copy in outs:
         copy.start()
@@ -1619,9 +1622,9 @@
     def project_slot(s):
         x = whole_rows(side, mine[s], other[s]).astype(BF16)
         xb[s] = x
-        qb[s] = ((nn(x, weight(0)) + table_row(vec, QUERY_BIAS, entries)) * SCALE).astype(BF16)
+        qb[s] = ((nn(x, weight(0)) + table[QUERY_BIAS : QUERY_BIAS + 1]) * SCALE).astype(BF16)
         kb[s] = nn(x, weight(1)).astype(BF16)
-        vb[s] = (nn(x, weight(2)) + table_row(vec, VALUE_BIAS, entries)).astype(BF16)
+        vb[s] = (nn(x, weight(2)) + table[VALUE_BIAS : VALUE_BIAS + 1]).astype(BF16)
         for i, (buf, out) in enumerate(((xb, x_ref), (qb, q_ref), (kb, k_ref), (vb, v_ref))):
             outs.append(pltpu.make_async_copy(buf.at[s], out.at[s], out_sem.at[2 + 4 * s + i]))
             outs[-1].start()
@@ -1670,13 +1673,14 @@
         out_shape=[
             sds(attn_shape, BF16),
             sds((2, nz, 2, 2, 2, hidden, D), BF16),
-            sds(vec_shape, F32),
+            sds((NVEC, D), F32),
             *[whole] * 5,
             sds(logs, F32),
         ],
         scratch_shapes=[
             pltpu.VMEM(attn_shape, BF16),
             pltpu.VMEM(vec_shape, F32),
+            pltpu.VMEM((NVEC, D), F32),
             half,
             half,
             *[pltpu.VMEM(whole.shape, BF16)] * 5,
@@ -2190,8 +2194,8 @@
             tokens,
         )
     attn, ffn = attn.reshape(4, D, D), ffn.reshape(2, FF, D)
-    table = table.reshape(nz * 8, VEC_TILE[0] * VEC_TILE[1])[:, :entries].reshape(NVEC, D)
     if not aligned:
+        table = table.reshape(nz * 8, VEC_TILE[0] * VEC_TILE[1])[:, :entries].reshape(NVEC, D)
         work = project(tokens, other, attn, table)
         work = [*work, *attend(*work[1:])]
     return attn, ffn, table, work

time: 316 us -> 314 us (level)
    unnamed x31 -> x30, local copies, waits for them, and re-layouts: 9.93 us -> 8.89 us
where the time goes in v4:
time: 314 us; the launch traced here: 311 us
  Pallas kernels  294 us (94%)
  local copies, waits for them, and re-layouts  8.9 us (3%)
  other arithmetic  6.36 us (2%)
    pallas_call x1, Pallas kernels, tail(): pl.pallas_call(functools.partial(tail_kernel, nz), in_specs=[SMEM, VMEM,...  87.1 us
    pallas_call x1, Pallas kernels, head(): pl.pallas_call(functools.partial(head_kernel, nz, entries), in_specs=[ANY...  74.7 us
    pallas_call x1, Pallas kernels, rows_part(): pl.pallas_call(rows_kernel, grid=(LOCAL,), in_specs=[SMEM, rows, rows, th...  58 us
    pallas_call x1, Pallas kernels, chain_back(): pl.pallas_call(chain_back_kernel, in_specs=[SMEM, VMEM] + [ANY] * 18, out...  55 us
    pallas_call x1, Pallas kernels, chain(): pl.pallas_call(chain_kernel, in_specs=[SMEM, VMEM] + [ANY] * 7, out_specs...  19.6 us
    unnamed x30, local copies, waits for them, and re-layouts  8.89 us

profile of v4, /device:TPU:1, one launch (start us, length us, event | category | flops | bytes accessed | tf_op | source)
XLA Modules:
  0.0 310.7 jit_solution(17029633692458687499)
XLA Ops:
  0.6 0.0 copy-start
  0.7 0.0 copy-start.4
  0.7 0.0 copy-start.10
  0.7 2.8 copy.29.tokens
  3.5 0.7 convert_bitcast_fusion.ffn_src
  4.2 0.0 copy-done.4
  4.2 0.7 convert_element_type.19.attn_src
  4.9 0.6 bitcast_convert_fusion.vec_src
  5.5 74.7 %head.1 = (bf16[4,4,2,2,48,768]{5,4,3,2,1,0:T(8,128)(2,1)}, bf16[2,4,2,2,2,96,768]{6,5,4,3,2,1,0:T(8,128)(2,1)}, f32[22,768]{1,0:T(8,128)}, bf16[2,512,768]{2,1,...) custom-call(bf16[4,48,384]{2,1,0:T(8,128)(2,1)} %convert_element_typ, ...), custom_call_target="tpu_custom_call" | custom-call | tf_op jit(solution)/shard_map/head/pallas_call | solution.py:1669
  80.2 0.0 copy-done.3
  80.3 1.3 copy.30.cot_ref.mine_ref
  81.6 19.6 %chain.1 = (bf16[2,512,768]{2,1,0:T(8,128)(2,1)}, bf16[2,512,768]{2,1,0:T(8,128)(2,1)}, bf16[2,512,768]{2,1,0:T(8,128)(2,1)}, bf16[2,512,768]{2,1,0:T(8,128)(2,1...) custom-call(s32[4]{0:T(128)} %refs_0_.1, ...), custom_call_target="tpu_custom_call", output_to_operand_aliasing={{0}: (4, {}), {1}: (5, {}), {2}: (6, {}), {3}: (7, {})} | custom-call | tf_op jit(solution)/shard_map/chain/pallas_call | solution.py:895
  101.2 58.0 %rows_part.1 = (bf16[2,251,768]{2,1,0:T(8,128)(2,1)}, bf16[2,251,768]{2,1,0:T(8,128)(2,1)}, bf16[2,512,768]{2,1,0:T(8,128)(2,1)}, bf16[2,512,3072]{2,1,0:T(8,128...) custom-call(s32[4]{0:T(128)} %refs_0_.1, ...), custom_call_target="tpu_custom_call" | custom-call | tf_op jit(solution)/shard_map/rows_part/pallas_call | solution.py:1130
  159.2 55.0 %chain_back.1 = (bf16[2,512,768]{2,1,0:T(8,128)(2,1)}, bf16[2,512,768]{2,1,0:T(8,128)(2,1)}, bf16[2,512,768]{2,1,0:T(8,128)(2,1)}, bf16[2,512,768]{2,1,0:T(8,128...) custom-call(s32[4]{0:T(128)} %refs_0_.1, ...), custom_call_target="tpu_custom_call", output_to_operand_aliasing={{0}: (18, {}), {1}: (19, {})} | custom-call | tf_op jit(solution)/shard_map/chain_back/pallas_call | solution.py:1482
  214.2 0.0 copy-start.5
  214.2 87.1 %tail.1 = (bf16[4,48,384]{2,1,0:T(8,128)(2,1)}, bf16[2,96,768]{2,1,0:T(8,128)(2,1)}, f32[28,768]{1,0:T(8,128)}, bf16[4,251,768]{2,1,0:T(8,128)(2,1)}) custom-call(s32[4]{0:T(128)} %refs_0_.1, f32[16,768]{1,0:T(8,128)} %get-tuple-element.79.refs_1_, f32[28,768]{1,0:T(8,128)} %get-tuple-element.80.refs_2_, bf16[2,4,2,2,2,96,768]{6,5,4,3,2,1,0:T(8,128)(2,1)} %bitcast.24, ...), custom_call_target="tpu_custom_call" | custom-call | tf_op jit(solution)/shard_map/tail/pallas_call | solution.py:2125
  301.4 0.0 copy-done.5
  301.4 0.0 copy-start.2
  301.4 2.7 multiply_add_fusion
  304.0 2.3 copy.33
  306.4 1.0 multiply_add_fusion.1
  307.5 0.7 multiply_add_fusion.2
  308.2 0.0 copy-done.1
  308.2 2.3 copy.32
  (20 shorter events, 0.0 us)
Async XLA Ops:
  0.6 2.8 copy-start
  0.7 3.6 %copy-start.4 = (f32[4,48,384]{2,1,0:T(8,128)S(1)}, f32[4,48,384]{2,1,0:T(8,128)}, u32[]{:S(2)}) copy-start(f32[4,48,384]{2,1,0:T(8,128)} %param.15) | copy-start | bytes 884740
  0.7 4.3 %copy-start.10 = (f32[528]{0:T(1024)S(1)}, f32[528]{0:T(1024)}, u32[]{:S(2)}) copy-start(f32[528]{0:T(1024)} %param.17) | copy-start | bytes 6340
  3.5 76.8 %copy-start.3 = (bf16[4,251,768]{2,0,1:T(4,128)(2,1)S(1)}, bf16[4,251,768]{2,0,1:T(4,128)(2,1)}, u32[]{:S(2)}) copy-start(bf16[4,251,768]{2,0,1:T(4,128)(2,1)} %param.14) | copy-start | bytes 4626436
  214.2 87.2 %copy-start.5 = (f32[2,768,96]{1,2,0:T(8,128)S(1)}, f32[2,768,96]{1,2,0:T(8,128)}, u32[]{:S(2)}) copy-start(f32[2,768,96]{1,2,0:T(8,128)} %param.22) | copy-start | bytes 1769476
  301.4 2.7 copy-start.2
  304.0 2.4 copy-start.6
  304.0 2.4 copy-start.7
  304.0 2.4 copy-start.8
  306.4 1.0 copy-start.9
  306.4 1.1 copy-start.11
  306.4 1.1 copy-start.12
  306.4 1.8 copy-start.1

commit v5 on v4

--- a/solution.py
+++ b/solution.py
@@ -1273,9 +1273,9 @@
 
     @pl.when(y == 0)
     def _():
+        for copy in reads + saved + loads[:0:-1] + loads[:1] + tile_reads:
+            copy.start()
         for copy in rows_in + chunk_reads(0) + chunk_reads(1):
-            copy.start()
-        for copy in reads + saved + loads[:0:-1] + loads[:1] + tile_reads:
             copy.start()
 
     pair_barrier(place)

time: 314 us -> 314 us (level)
  no operation moved by 1% of the time
where the time goes in v5:
time: 314 us; the launch traced here: 311 us
  Pallas kernels  294 us (94%)
  local copies, waits for them, and re-layouts  8.9 us (3%)
  other arithmetic  6.36 us (2%)
    pallas_call x1, Pallas kernels, tail(): pl.pallas_call(functools.partial(tail_kernel, nz), in_specs=[SMEM, VMEM,...  87.1 us
    pallas_call x1, Pallas kernels, head(): pl.pallas_call(functools.partial(head_kernel, nz, entries), in_specs=[ANY...  74.7 us
    pallas_call x1, Pallas kernels, rows_part(): pl.pallas_call(rows_kernel, grid=(LOCAL,), in_specs=[SMEM, rows, rows, th...  58 us
    pallas_call x1, Pallas kernels, chain_back(): pl.pallas_call(chain_back_kernel, in_specs=[SMEM, VMEM] + [ANY] * 18, out...  55 us
    pallas_call x1, Pallas kernels, chain(): pl.pallas_call(chain_kernel, in_specs=[SMEM, VMEM] + [ANY] * 7, out_specs...  19.6 us
    unnamed x30, local copies, waits for them, and re-layouts  8.89 us

profile of v5, /device:TPU:1, one launch (start us, length us, event | category | flops | bytes accessed | tf_op | source)
XLA Modules:
  0.0 310.7 jit_solution(15524959972282067081)
XLA Ops:
  0.6 0.0 copy-start
  0.7 0.0 copy-start.4
  0.7 0.0 copy-start.10
  0.7 2.8 copy.29.tokens
  3.5 0.7 convert_bitcast_fusion.ffn_src
  4.2 0.0 copy-done.4
  4.2 0.7 convert_element_type.19.attn_src
  4.9 0.6 bitcast_convert_fusion.vec_src
  5.5 74.7 %head.1 = (bf16[4,4,2,2,48,768]{5,4,3,2,1,0:T(8,128)(2,1)}, bf16[2,4,2,2,2,96,768]{6,5,4,3,2,1,0:T(8,128)(2,1)}, f32[22,768]{1,0:T(8,128)}, bf16[2,512,768]{2,1,...) custom-call(bf16[4,48,384]{2,1,0:T(8,128)(2,1)} %convert_element_typ, ...), custom_call_target="tpu_custom_call" | custom-call | tf_op jit(solution)/shard_map/head/pallas_call | solution.py:1669
  80.2 0.0 copy-done.3
  80.3 1.3 copy.30.cot_ref.mine_ref
  81.6 19.6 %chain.1 = (bf16[2,512,768]{2,1,0:T(8,128)(2,1)}, bf16[2,512,768]{2,1,0:T(8,128)(2,1)}, bf16[2,512,768]{2,1,0:T(8,128)(2,1)}, bf16[2,512,768]{2,1,0:T(8,128)(2,1...) custom-call(s32[4]{0:T(128)} %refs_0_.1, ...), custom_call_target="tpu_custom_call", output_to_operand_aliasing={{0}: (4, {}), {1}: (5, {}), {2}: (6, {}), {3}: (7, {})} | custom-call | tf_op jit(solution)/shard_map/chain/pallas_call | solution.py:895
  101.2 58.0 %rows_part.1 = (bf16[2,251,768]{2,1,0:T(8,128)(2,1)}, bf16[2,251,768]{2,1,0:T(8,128)(2,1)}, bf16[2,512,768]{2,1,0:T(8,128)(2,1)}, bf16[2,512,3072]{2,1,0:T(8,128...) custom-call(s32[4]{0:T(128)} %refs_0_.1, ...), custom_call_target="tpu_custom_call" | custom-call | tf_op jit(solution)/shard_map/rows_part/pallas_call | solution.py:1130
  159.2 55.0 %chain_back.1 = (bf16[2,512,768]{2,1,0:T(8,128)(2,1)}, bf16[2,512,768]{2,1,0:T(8,128)(2,1)}, bf16[2,512,768]{2,1,0:T(8,128)(2,1)}, bf16[2,512,768]{2,1,0:T(8,128...) custom-call(s32[4]{0:T(128)} %refs_0_.1, ...), custom_call_target="tpu_custom_call", output_to_operand_aliasing={{0}: (18, {}), {1}: (19, {})} | custom-call | tf_op jit(solution)/shard_map/chain_back/pallas_call | solution.py:1482
  214.2 0.0 copy-start.5
  214.2 87.1 %tail.1 = (bf16[4,48,384]{2,1,0:T(8,128)(2,1)}, bf16[2,96,768]{2,1,0:T(8,128)(2,1)}, f32[28,768]{1,0:T(8,128)}, bf16[4,251,768]{2,1,0:T(8,128)(2,1)}) custom-call(s32[4]{0:T(128)} %refs_0_.1, f32[16,768]{1,0:T(8,128)} %get-tuple-element.79.refs_1_, f32[28,768]{1,0:T(8,128)} %get-tuple-element.80.refs_2_, bf16[2,4,2,2,2,96,768]{6,5,4,3,2,1,0:T(8,128)(2,1)} %bitcast.24, ...), custom_call_target="tpu_custom_call" | custom-call | tf_op jit(solution)/shard_map/tail/pallas_call | solution.py:2125
  301.4 0.0 copy-done.5
  301.4 0.0 copy-start.2
  301.4 2.7 multiply_add_fusion
  304.0 2.3 copy.33
  306.4 1.0 multiply_add_fusion.1
  307.5 0.7 multiply_add_fusion.2
  308.2 0.0 copy-done.1
  308.2 2.3 copy.32
  (20 shorter events, 0.0 us)
Async XLA Ops:
  0.6 2.8 copy-start
  0.7 3.6 %copy-start.4 = (f32[4,48,384]{2,1,0:T(8,128)S(1)}, f32[4,48,384]{2,1,0:T(8,128)}, u32[]{:S(2)}) copy-start(f32[4,48,384]{2,1,0:T(8,128)} %param.15) | copy-start | bytes 884740
  0.7 4.3 %copy-start.10 = (f32[528]{0:T(1024)S(1)}, f32[528]{0:T(1024)}, u32[]{:S(2)}) copy-start(f32[528]{0:T(1024)} %param.17) | copy-start | bytes 6340
  3.5 76.8 %copy-start.3 = (bf16[4,251,768]{2,0,1:T(4,128)(2,1)S(1)}, bf16[4,251,768]{2,0,1:T(4,128)(2,1)}, u32[]{:S(2)}) copy-start(bf16[4,251,768]{2,0,1:T(4,128)(2,1)} %param.14) | copy-start | bytes 4626436
  214.2 87.2 %copy-start.5 = (f32[2,768,96]{1,2,0:T(8,128)S(1)}, f32[2,768,96]{1,2,0:T(8,128)}, u32[]{:S(2)}) copy-start(f32[2,768,96]{1,2,0:T(8,128)} %param.22) | copy-start | bytes 1769476
  301.4 2.7 copy-start.2
  304.0 2.4 copy-start.6
  304.0 2.4 copy-start.7
  304.0 2.4 copy-start.8
  306.4 1.0 copy-start.9
  306.4 1.1 copy-start.11
  306.4 1.1 copy-start.12
  306.4 1.8 copy-start.1
